TPU v7x, 32 devices: a whole 2x2x4 slice. The times are simulated.
32 devices in a mesh: expert: 16 (over z, y, x), shard: 2 (over core).
Axes of the slice: x: 2, y: 2, z: 4, core: 2. Of those that a mesh axis runs over, the one named last changes fastest.
Arguments:
- hidden_in: bfloat16 [4096, 1024], P(('expert', 'shard')), may hold values from -6 to 6
- doc_lengths: int32 [32, 3], P('expert'), may hold values from 1 to 96, 128 in all within a row
- routes: int32 [4096, 8], P(('expert', 'shard')), may hold values from 0 to 15, all different within a row; in each aligned block of 128 rows (0 to 127, 128 to 255, ...) at most 68 rows name the same one
- attn_norm_gain: float32 [1024], replicated, may hold values from 0.5 to 1.5
- query_weight: bfloat16 [1024, 1024], P('shard'), may hold values from -0.75 to 0.75
- key_weight: bfloat16 [1024, 512], P('shard'), may hold values from -0.75 to 0.75
- value_weight: bfloat16 [1024, 512], P('shard'), may hold values from -0.75 to 0.75
- output_weight: bfloat16 [1024, 1024], P('shard'), may hold values from -0.75 to 0.75
- router_weight: bfloat16 [1024, 16], P('shard'), may hold values from -0.09375 to 0.09375
- moe_norm_gain: float32 [1024], replicated, may hold values from 0.5 to 1.5
- gate_weight: bfloat16 [16, 1024, 512], P('expert'), may hold values from -0.1875 to 0.1875
- up_weight: bfloat16 [16, 1024, 512], P('expert'), may hold values from -0.75 to 0.75
- down_weight: bfloat16 [16, 512, 1024], P('expert'), may hold values from -1.5 to 1.5
- cotangent: bfloat16 [4096, 1024], P(('expert', 'shard')), may hold values from -6 to 6
Outputs:
- layer_out: bfloat16 [4096, 1024], P(('expert', 'shard'))
- input_grad: float32 [4096, 1024], P(('expert', 'shard'))
- attn_norm_grad: float32 [1024], P('shard')
- query_grad: float32 [1024, 1024], P('shard')
- key_grad: float32 [1024, 512], P('shard')
- value_grad: float32 [1024, 512], P('shard')
- output_grad: float32 [1024, 1024], P('shard')
- router_grad: float32 [1024, 16], P('shard')
- moe_norm_grad: float32 [1024], P('shard')
- gate_grad: float32 [16, 1024, 512], P('expert', 'shard')
- up_grad: float32 [16, 1024, 512], P('expert', 'shard')
- down_grad: float32 [16, 512, 1024], P('expert', 'shard')
Inputs may be any that keep to these rules, and one draw needn't show every extreme that they name: `routes`: in the 128 tokens of one device no expert is named more than 68 times, a bound that some block reaches; a token names 8 different experts. `doc_lengths`: each row sums to 128; its longest document has 128 - 128 // 4 tokens.
All inputs are finite; a program needn't handle non-finite values.
Results may differ from a plain program's by a relative error of at most 0.02.
Values may be sent and summed in bfloat16 or wider, within the bound.
A program may use at most 128 MiB of HBM per device.

v0:
```python
import jax
import jax.numpy as jnp
from jax import lax
from jax.sharding import PartitionSpec as P

HEADS = 16
KV_HEADS = 8
HEAD_DIM = 64
TOP = 8


epsilon = 1e-06
res_scale = 0.22
att_scale = 0.015625
rope_base = 10000.0
masked_score = -1e30


def rms_norm(values, gain):
    return values * lax.rsqrt(jnp.mean(values * values, -1, keepdims=True) + epsilon) * gain


def doc_layout(lengths, positions):
    doc_ends = jnp.cumsum(lengths)
    past_end = positions[:, None] >= doc_ends[None, :]
    doc_index = jnp.sum(past_end.astype(jnp.int32), 1)
    doc_start = jnp.sum(jnp.where(past_end, lengths[None, :], 0), 1)
    return (doc_index, positions - doc_start)


def rope_tables(offsets):
    half_size = HEAD_DIM // 2
    frequency = rope_base ** (-2.0 * jnp.arange(half_size).astype(jnp.float32) / HEAD_DIM)
    angles = offsets.astype(jnp.float32)[:, None] * frequency[None, :]
    return (jnp.cos(angles), jnp.sin(angles))


def rotate(values, cos_table, sin_table, inverse):
    row_count = values.shape[0]
    shaped = values.reshape(row_count, -1, HEAD_DIM)
    half_size = HEAD_DIM // 2
    front_part = shaped[:, :, :half_size]
    back_part = shaped[:, :, half_size:]
    cos_wide = cos_table[:, None, :]
    sin_wide = sin_table[:, None, :]
    if inverse:
        sin_wide = -sin_wide
    turned = jnp.concatenate(
        [
            front_part * cos_wide - back_part * sin_wide,
            back_part * cos_wide + front_part * sin_wide,
        ],
        -1,
    )
    return turned.reshape(row_count, -1)


def on_device(
    hidden_in,
    doc_lengths,
    routes,
    attn_norm_gain,
    query_weight,
    key_weight,
    value_weight,
    output_weight,
    router_weight,
    moe_norm_gain,
    gate_weight,
    up_weight,
    down_weight,
    cotangent,
):
    tok_count = hidden_in.shape[0]
    model_width = hidden_in.shape[1]
    shard_index = lax.axis_index("shard")
    query_full, key_full, value_full, output_full, router_full = (
        lax.all_gather(query_weight, "shard", axis=0, tiled=True),
        lax.all_gather(key_weight, "shard", axis=0, tiled=True),
        lax.all_gather(value_weight, "shard", axis=0, tiled=True),
        lax.all_gather(output_weight, "shard", axis=0, tiled=True),
        lax.all_gather(router_weight, "shard", axis=0, tiled=True),
    )
    expert_count = router_full.shape[1]
    capacity = 17 * tok_count * TOP // (16 * expert_count)
    sub_rows = tok_count // 2
    seq_len = sub_rows * lax.axis_size("shard")
    group_ratio = HEADS // KV_HEADS
    input_float = hidden_in.astype(jnp.float32)
    normed_one = rms_norm(input_float, attn_norm_gain).astype(jnp.bfloat16)
    query_raw = jnp.dot(normed_one, query_full, preferred_element_type=jnp.float32)
    key_raw = jnp.dot(normed_one, key_full, preferred_element_type=jnp.float32)
    value_raw = jnp.dot(normed_one, value_full, preferred_element_type=jnp.float32)
    own_positions = shard_index * sub_rows + jnp.arange(sub_rows, dtype=jnp.int32)
    seq_positions = jnp.arange(seq_len, dtype=jnp.int32)
    layout_both = jax.vmap(doc_layout, in_axes=(0, None))
    query_docs, query_offsets = layout_both(doc_lengths, own_positions)
    key_docs, unused_offsets = layout_both(doc_lengths, seq_positions)
    cos_table, sin_table = rope_tables(query_offsets.reshape(-1))
    query_rot = rotate(query_raw, cos_table, sin_table, False).astype(jnp.bfloat16)
    key_rot = rotate(key_raw, cos_table, sin_table, False).astype(jnp.bfloat16)
    value_low = value_raw.astype(jnp.bfloat16)
    key_group, value_group = (
        lax.all_gather(key_rot.reshape(2, sub_rows, -1), "shard", axis=1, tiled=True),
        lax.all_gather(value_low.reshape(2, sub_rows, -1), "shard", axis=1, tiled=True),
    )
    allowed = (
        (own_positions[None, :, None] >= seq_positions[None, None, :])
        & (query_docs[:, :, None] == key_docs[:, None, :])
    )[:, None, None]
    query_heads = query_rot.reshape(2, sub_rows, KV_HEADS, group_ratio, HEAD_DIM)
    key_heads = key_group.reshape(2, seq_len, KV_HEADS, HEAD_DIM)
    value_heads = value_group.reshape(2, seq_len, KV_HEADS, HEAD_DIM)

    def attention_scores():
        raw_scores = (
            jnp.einsum(
                "btkgd,bskd->bkgts", query_heads, key_heads, preferred_element_type=jnp.float32
            )
            * att_scale
        )
        return jnp.where(allowed, raw_scores, masked_score)

    scores = attention_scores()
    top_score = jnp.max(scores, -1, keepdims=True)
    exp_scores = jnp.exp(scores - top_score)
    exp_total = jnp.sum(exp_scores, -1, keepdims=True)
    log_total = top_score + jnp.log(exp_total)
    probs_low = (exp_scores / exp_total).astype(jnp.bfloat16)
    attn_mix = jnp.einsum(
        "bkgts,bskd->btkgd", probs_low, value_heads, preferred_element_type=jnp.float32
    )
    attn_low = attn_mix.reshape(tok_count, -1).astype(jnp.bfloat16)
    branch = jnp.dot(attn_low, output_full, preferred_element_type=jnp.float32)
    middle = input_float + res_scale * branch
    normed_two = rms_norm(middle, moe_norm_gain).astype(jnp.bfloat16)
    logits = jnp.dot(normed_two, router_full, preferred_element_type=jnp.float32)
    route_picks = (
        routes[:, :, None] == jnp.arange(expert_count, dtype=jnp.int32)[None, None, :]
    ).astype(jnp.float32)
    chosen = jnp.sum(route_picks * logits[:, None, :], -1)
    top_chosen = jnp.max(chosen, -1, keepdims=True)
    gate_exp = jnp.exp(chosen - top_chosen)
    gate_probs = gate_exp / jnp.sum(gate_exp, -1, keepdims=True)
    slot_expert = routes.reshape(-1)
    slot_hot = (slot_expert[:, None] == jnp.arange(expert_count, dtype=jnp.int32)[None, :]).astype(
        jnp.int32
    )
    slot_place = jnp.sum((jnp.cumsum(slot_hot, 0) - slot_hot) * slot_hot, 1)
    send_rows = (
        jnp.zeros((expert_count, capacity, model_width), jnp.bfloat16)
        .at[slot_expert, slot_place]
        .set(jnp.repeat(normed_two, TOP, 0))
    )
    gate_matrix = gate_weight[0]
    up_matrix = up_weight[0]
    down_matrix = down_weight[0]
    hidden_units = gate_matrix.shape[1]
    arrived_rows = lax.all_to_all(send_rows, "expert", split_axis=0, concat_axis=0, tiled=True)
    source_count = arrived_rows.shape[0]
    slot_count = arrived_rows.shape[1]
    flat_rows = arrived_rows.reshape(-1, model_width)
    gate_pre = jnp.dot(flat_rows, gate_matrix, preferred_element_type=jnp.float32)
    up_pre = jnp.dot(flat_rows, up_matrix, preferred_element_type=jnp.float32)
    inner = (jax.nn.silu(gate_pre) * up_pre).astype(jnp.bfloat16)
    result = jnp.dot(inner, down_matrix, preferred_element_type=jnp.float32).astype(jnp.bfloat16)
    returned = lax.all_to_all(
        result.reshape(source_count, slot_count, model_width),
        "expert",
        split_axis=0,
        concat_axis=0,
        tiled=True,
    )
    dispatched = (
        returned,
        arrived_rows,
        gate_pre.reshape(source_count, slot_count, hidden_units),
        up_pre.reshape(source_count, slot_count, hidden_units),
    )
    returned = dispatched[0]
    arrived = dispatched[1]
    slot_out = (
        returned[slot_expert, slot_place].reshape(tok_count, TOP, model_width).astype(jnp.float32)
    )
    mixture = jnp.sum(gate_probs[:, :, None] * slot_out, 1)
    layer_out = (middle + res_scale * mixture).astype(jnp.bfloat16)
    grad_out = cotangent.astype(jnp.float32)
    grad_mix = res_scale * grad_out
    grad_gates = jnp.sum(grad_mix[:, None, :] * slot_out, -1)
    slot_grads = (
        (gate_probs[:, :, None] * grad_mix[:, None, :])
        .astype(jnp.bfloat16)
        .reshape(-1, model_width)
    )
    send_grads = (
        jnp.zeros((expert_count, capacity, model_width), jnp.bfloat16)
        .at[slot_expert, slot_place]
        .set(slot_grads)
    )
    arrived_grads = lax.all_to_all(send_grads, "expert", split_axis=0, concat_axis=0, tiled=True)
    flat_rows = arrived.reshape(-1, model_width)
    gate_pre = dispatched[2].reshape(-1, hidden_units)
    up_pre = dispatched[3].reshape(-1, hidden_units)
    sigmoid_gate = jax.nn.sigmoid(gate_pre)
    activated = gate_pre * sigmoid_gate
    inner = (activated * up_pre).astype(jnp.bfloat16)
    flat_grads = arrived_grads.reshape(-1, model_width)
    down_wgrad = jnp.einsum("rf,rd->fd", inner, flat_grads, preferred_element_type=jnp.float32)
    inner_grad = jnp.einsum(
        "rd,fd->rf", flat_grads, down_matrix, preferred_element_type=jnp.float32
    )
    gate_pregrad = (
        inner_grad * up_pre * sigmoid_gate * (1.0 + gate_pre * (1.0 - sigmoid_gate))
    ).astype(jnp.bfloat16)
    up_pregrad = (inner_grad * activated).astype(jnp.bfloat16)
    gate_wgrad = jnp.einsum(
        "rd,rf->df", flat_rows, gate_pregrad, preferred_element_type=jnp.float32
    )
    up_wgrad = jnp.einsum("rd,rf->df", flat_rows, up_pregrad, preferred_element_type=jnp.float32)
    row_grads = (
        jnp.einsum("rf,df->rd", gate_pregrad, gate_matrix, preferred_element_type=jnp.float32)
        + jnp.einsum("rf,df->rd", up_pregrad, up_matrix, preferred_element_type=jnp.float32)
    ).astype(jnp.bfloat16)
    back_grads = lax.all_to_all(
        row_grads.reshape(expert_count, capacity, model_width),
        "expert",
        split_axis=0,
        concat_axis=0,
        tiled=True,
    )
    normed_two_grad = jnp.sum(
        back_grads[slot_expert, slot_place]
        .reshape(tok_count, TOP, model_width)
        .astype(jnp.float32),
        1,
    )
    gate_dot = jnp.sum(gate_probs * grad_gates, 1, keepdims=True)
    chosen_grad = gate_probs * (grad_gates - gate_dot)
    logit_grad = jnp.sum(route_picks * chosen_grad[:, :, None], 1).astype(jnp.bfloat16)
    router_wgrad = jnp.einsum(
        "td,te->de", normed_two, logit_grad, preferred_element_type=jnp.float32
    )
    normed_two_grad = normed_two_grad + jnp.einsum(
        "te,de->td", logit_grad, router_full, preferred_element_type=jnp.float32
    )
    unused_value, second_pull = jax.vjp(rms_norm, middle, moe_norm_gain)
    middle_from_norm, moe_gain_grad = second_pull(normed_two_grad)
    middle_grad = grad_out + middle_from_norm
    branch_grad = (res_scale * middle_grad).astype(jnp.bfloat16)
    output_wgrad = jnp.einsum(
        "tq,td->qd", attn_low, branch_grad, preferred_element_type=jnp.float32
    )
    attn_grad = jnp.einsum(
        "td,qd->tq", branch_grad, output_full, preferred_element_type=jnp.float32
    ).astype(jnp.bfloat16)
    attn_grad = attn_grad.reshape(2, sub_rows, KV_HEADS, group_ratio, HEAD_DIM)
    probs = jnp.exp(attention_scores() - log_total)
    probs_low = probs.astype(jnp.bfloat16)
    prob_grad = jnp.einsum(
        "btkgd,bskd->bkgts", attn_grad, value_heads, preferred_element_type=jnp.float32
    )
    value_part = jnp.einsum(
        "bkgts,btkgd->bskd", probs_low, attn_grad, preferred_element_type=jnp.float32
    )
    score_grad = (probs * (prob_grad - jnp.sum(probs * prob_grad, -1, keepdims=True))).astype(
        jnp.bfloat16
    )
    query_rot_grad = att_scale * jnp.einsum(
        "bkgts,bskd->btkgd", score_grad, key_heads, preferred_element_type=jnp.float32
    )
    key_part = att_scale * jnp.einsum(
        "bkgts,btkgd->bskd", score_grad, query_heads, preferred_element_type=jnp.float32
    )
    key_rot_grad, value_pre = (
        lax.psum_scatter(
            key_part.reshape(2, seq_len, -1).astype(jnp.bfloat16),
            "shard",
            scatter_dimension=1,
            tiled=True,
        ).astype(jnp.float32),
        lax.psum_scatter(
            value_part.reshape(2, seq_len, -1).astype(jnp.bfloat16),
            "shard",
            scatter_dimension=1,
            tiled=True,
        ).astype(jnp.float32),
    )
    query_pre_grad = rotate(
        query_rot_grad.reshape(tok_count, -1), cos_table, sin_table, True
    ).astype(jnp.bfloat16)
    key_pre_grad = rotate(key_rot_grad.reshape(tok_count, -1), cos_table, sin_table, True).astype(
        jnp.bfloat16
    )
    value_pre_grad = value_pre.reshape(tok_count, -1).astype(jnp.bfloat16)
    query_wgrad = jnp.einsum(
        "td,tq->dq", normed_one, query_pre_grad, preferred_element_type=jnp.float32
    )
    key_wgrad = jnp.einsum(
        "td,tq->dq", normed_one, key_pre_grad, preferred_element_type=jnp.float32
    )
    value_wgrad = jnp.einsum(
        "td,tq->dq", normed_one, value_pre_grad, preferred_element_type=jnp.float32
    )
    normed_one_grad = (
        jnp.einsum("tq,dq->td", query_pre_grad, query_full, preferred_element_type=jnp.float32)
        + jnp.einsum("tq,dq->td", key_pre_grad, key_full, preferred_element_type=jnp.float32)
        + jnp.einsum("tq,dq->td", value_pre_grad, value_full, preferred_element_type=jnp.float32)
    )
    unused_first, first_pull = jax.vjp(rms_norm, input_float, attn_norm_gain)
    input_from_norm, attn_gain_grad = first_pull(normed_one_grad)
    input_grad = middle_grad + input_from_norm
    shard_sums = (
        lax.psum_scatter(
            query_wgrad.astype(jnp.bfloat16), "shard", scatter_dimension=0, tiled=True
        ).astype(jnp.float32),
        lax.psum_scatter(
            key_wgrad.astype(jnp.bfloat16), "shard", scatter_dimension=0, tiled=True
        ).astype(jnp.float32),
        lax.psum_scatter(
            value_wgrad.astype(jnp.bfloat16), "shard", scatter_dimension=0, tiled=True
        ).astype(jnp.float32),
        lax.psum_scatter(
            output_wgrad.astype(jnp.bfloat16), "shard", scatter_dimension=0, tiled=True
        ).astype(jnp.float32),
        lax.psum_scatter(
            router_wgrad.astype(jnp.bfloat16), "shard", scatter_dimension=0, tiled=True
        ).astype(jnp.float32),
        lax.psum_scatter(
            attn_gain_grad.astype(jnp.bfloat16), "shard", scatter_dimension=0, tiled=True
        ).astype(jnp.float32),
        lax.psum_scatter(
            moe_gain_grad.astype(jnp.bfloat16), "shard", scatter_dimension=0, tiled=True
        ).astype(jnp.float32),
    )
    totals = (
        lax.psum(shard_sums[0].astype(jnp.bfloat16), "expert").astype(jnp.float32),
        lax.psum(shard_sums[1].astype(jnp.bfloat16), "expert").astype(jnp.float32),
        lax.psum(shard_sums[2].astype(jnp.bfloat16), "expert").astype(jnp.float32),
        lax.psum(shard_sums[3].astype(jnp.bfloat16), "expert").astype(jnp.float32),
        lax.psum(shard_sums[4].astype(jnp.bfloat16), "expert").astype(jnp.float32),
        lax.psum(shard_sums[5].astype(jnp.bfloat16), "expert").astype(jnp.float32),
        lax.psum(shard_sums[6].astype(jnp.bfloat16), "expert").astype(jnp.float32),
    )
    expert_sums = (
        lax.psum_scatter(
            gate_wgrad.astype(jnp.bfloat16), "shard", scatter_dimension=0, tiled=True
        ).astype(jnp.float32),
        lax.psum_scatter(
            up_wgrad.astype(jnp.bfloat16), "shard", scatter_dimension=0, tiled=True
        ).astype(jnp.float32),
        lax.psum_scatter(
            down_wgrad.astype(jnp.bfloat16), "shard", scatter_dimension=0, tiled=True
        ).astype(jnp.float32),
    )
    return (
        layer_out,
        input_grad,
        totals[5],
        totals[0],
        totals[1],
        totals[2],
        totals[3],
        totals[4],
        totals[6],
        expert_sums[0][None],
        expert_sums[1][None],
        expert_sums[2][None],
    )


def solution(mesh):
    return jax.shard_map(
        on_device,
        mesh=mesh,
        in_specs=(
            P(("expert", "shard"), None),
            P("expert", None),
            P(("expert", "shard"), None),
            P(),
            P("shard", None),
            P("shard", None),
            P("shard", None),
            P("shard", None),
            P("shard", None),
            P(),
            P("expert", None, None),
            P("expert", None, None),
            P("expert", None, None),
            P(("expert", "shard"), None),
        ),
        out_specs=(
            P(("expert", "shard"), None),
            P(("expert", "shard"), None),
            P("shard"),
            P("shard", None),
            P("shard", None),
            P("shard", None),
            P("shard", None),
            P("shard", None),
            P("shard"),
            P("expert", "shard", None),
            P("expert", "shard", None),
            P("expert", "shard", None),
        ),
        check_vma=False,
    )
```

profile of v0, /device:TPU:0, one launch (start us, length us, event | category | flops | bytes accessed | tf_op | source)
XLA Modules:
  0.0 651.7 jit_solution(12679179893997861775)
XLA Ops:
  11.9 4.5 reduce-window.6
  18.5 2.9 all-gather.5.cloned.1.call-done
  21.5 1.6 convolution_convert_fusion.10
  23.0 2.0 all_gather.22
  25.2 8.0 %all-gather.7.cloned.1.call-done = bf16[1024,512]{1,0:T(8,128)(2,1)} async-done(((bf16[512,512]{1,0:T(8,128)(2,1)}), bf16[1024,512]{1,0:T(8,128)(2,1)}) %all-gather.7.cloned.1.call-update) | async-done | bytes 1048592 | tf_op jit(solution)/shard_map/all_gather | solution.py:79
  33.2 1.8 fusion.66
  35.4 2.0 all_gather.24
  37.6 8.9 %all-gather.9.cloned.1.call-done = bf16[1024,1024]{1,0:T(8,128)(2,1)} async-done(((bf16[512,1024]{1,0:T(8,128)(2,1)}), bf16[1024,1024]{1,0:T(8,128)(2,1)}) %all-gather.9.cloned.1.call-update) | async-done | bytes 2097168 | tf_op jit(solution)/shard_map/all_gather | solution.py:78
  46.5 2.6 fusion.64
  53.4 6.3 all-gather.11.cloned.1.call-done
  59.7 2.2 multiply_reduce_fusion.3
  63.5 6.3 scatter_custom_fusion
  69.8 2.7 copy.159
  72.5 7.0 %all-to-all-start = ((bf16[16,68,1024]{2,1,0:T(8,128)(2,1)}), bf16[16,68,1024]{2,1,0:T(8,128)(2,1)}, u32[]{:S(2)}, u32[]{:S(2)}) async-start(bf16[16,68,1024]{2,1,0:T(8,128)(2,1)} %copy.159), calls=%async_computation | async-start | bytes 4718592 | tf_op jit(solution)/shard_map/all_to_all | solution.py:159
  79.5 2.1 all_gather.27
  85.2 7.0 %scatter_custom_fusion.1 = bf16[1088,1024]{1,0:T(8,128)(2,1)S(1)} fusion(s32[1024]{0:T(1024)} %broadcast_select_fusion, f32[128,1024]{1,0:T(8,128)} %convert_multiply_fusion.6, f32[1024]{0:T(1024)} %div.73, bf16[]{:T(256)} %constant.53.clone.1), kind=kCustom, calls=%fused_computation.19 | custom fusion | flops 2097152 | bytes 2757120
  92.3 2.7 copy.162
  95.0 32.3 %all-to-all-done = bf16[16,68,1024]{2,1,0:T(8,128)(2,1)} async-done(((bf16[16,68,1024]{2,1,0:T(8,128)(2,1)}), bf16[16,68,1024]{2,1,0:T(8,128)(2,1)}, u32[]{:S(2)}, u32[]{:S(2)}) %all-to-all-start) | async-done | bytes 2228256 | tf_op jit(solution)/shard_map/all_to_all | solution.py:159
  127.2 11.9 %all-to-all-start.2 = ((bf16[16,68,1024]{2,1,0:T(8,128)(2,1)}), bf16[16,68,1024]{2,1,0:T(8,128)(2,1)}, u32[]{:S(2)}, u32[]{:S(2)}) async-start(bf16[16,68,1024]{2,1,0:T(8,128)(2,1)} %copy.162), calls=%async_computation.2 | async-start | bytes 4718592 | tf_op jit(solution)/shard_map/all_to_all | solution.py:200
  139.1 2.6 reshape.439
  141.7 4.8 fusion.25
  146.6 2.7 fusion.29
  149.3 37.0 %all-to-all-done.2 = bf16[16,68,1024]{2,1,0:T(8,128)(2,1)} async-done(((bf16[16,68,1024]{2,1,0:T(8,128)(2,1)}), bf16[16,68,1024]{2,1,0:T(8,128)(2,1)}, u32[]{:S(2)}, u32[]{:S(2)}) %all-to-all-start.2) | async-done | bytes 2228256 | tf_op jit(solution)/shard_map/all_to_all | solution.py:200
  186.3 2.6 reshape.441
  188.9 6.8 %multiply_convert_fusion = (bf16[1088,512]{1,0:T(8,128)(2,1)}, bf16[1088,512]{1,0:T(8,128)(2,1)}, bf16[1088,512]{1,0:T(8,128)(2,1)S(1)}) fusion(f32[1088,512]{1,0:T(8,128)} %fusion.29, f32[1088,512]{1,0:T(8,128)} %fusion.25, bf16[1088,1024]{1,0:T(8,128)(2,1)S(1)} %reshape.441, bf16[1,512,1024]{2,1,0:T(8,128)(2,1)S(1)} %copy-done), kind=kOutput, calls=%fused_computation.14 | convolution fusion | flops 1149206528 | bytes 11075584 | tf_op jit(solution)/shard_map/rd,fd->rf/dot_general | solution.py:209
  198.1 2.1 reshape.440
  200.2 20.6 %all-to-all-start.1 = ((bf16[16,68,1024]{2,1,0:T(8,128)(2,1)}), bf16[16,68,1024]{2,1,0:T(8,128)(2,1)}, u32[]{:S(2)}, u32[]{:S(2)}) async-start(bf16[16,68,1024]{2,1,0:T(8,128)(2,1)} %reshape.440), calls=%async_computation.1 | async-start | bytes 4718592 | tf_op jit(solution)/shard_map/all_to_all | solution.py:167
  222.4 1.4 fusion.3
  223.8 2.1 reshape.442
  225.9 42.0 %all-to-all-done.1 = bf16[16,68,1024]{2,1,0:T(8,128)(2,1)} async-done(((bf16[16,68,1024]{2,1,0:T(8,128)(2,1)}), bf16[16,68,1024]{2,1,0:T(8,128)(2,1)}, u32[]{:S(2)}, u32[]{:S(2)}) %all-to-all-start.1) | async-done | bytes 2228256 | tf_op jit(solution)/shard_map/all_to_all | solution.py:167
  267.9 10.7 %all-to-all-start.3 = ((bf16[16,68,1024]{2,1,0:T(8,128)(2,1)}), bf16[16,68,1024]{2,1,0:T(8,128)(2,1)}, u32[]{:S(2)}, u32[]{:S(2)}) async-start(bf16[16,68,1024]{2,1,0:T(8,128)(2,1)} %reshape.442), calls=%async_computation.3 | async-start | bytes 4718592 | tf_op jit(solution)/shard_map/all_to_all | solution.py:224
  279.2 2.9 copy.160
  282.1 15.2 %gather_fusion = bf16[1024,1024]{1,0:T(8,128)(2,1)} fusion(bf16[16,68,1024]{2,0,1:T(8,128)(2,1)S(1)} %copy.160, s32[1024]{0:T(1024)S(1)} %bitcast.165), kind=kCustom, calls=%fused_computation | custom fusion | bytes 4202496 | tf_op jit(solution)/shard_map/gather | solution.py:183
  297.3 3.3 fusion.1
  300.7 24.9 %all-to-all-done.3 = bf16[16,68,1024]{2,1,0:T(8,128)(2,1)} async-done(((bf16[16,68,1024]{2,1,0:T(8,128)(2,1)}), bf16[16,68,1024]{2,1,0:T(8,128)(2,1)}, u32[]{:S(2)}, u32[]{:S(2)}) %all-to-all-start.3) | async-done | bytes 2228256 | tf_op jit(solution)/shard_map/all_to_all | solution.py:224
  325.6 2.9 copy.163
  328.5 15.2 %gather_fusion.1 = bf16[1024,1024]{1,0:T(8,128)(2,1)} fusion(bf16[16,68,1024]{2,0,1:T(8,128)(2,1)S(1)} %copy.163, s32[1024]{0:T(1024)S(1)} %bitcast.166), kind=kCustom, calls=%fused_computation.1 | custom fusion | bytes 4202496 | tf_op jit(solution)/shard_map/gather | solution.py:232
  343.7 3.1 convert_reduce_fusion
  351.8 1.8 multiply_reduce_fusion
  353.5 1.9 copy.173
  358.1 10.1 %reduce-scatter.13.cloned.1.call-done = bf16[2,64,512]{2,1,0:T(8,128)(2,1)} async-done(((bf16[2,128,512]{2,1,0:T(8,128)(2,1)}), bf16[2,64,512]{2,1,0:T(8,128)(2,1)}) %reduce-scatter.13.cloned.1.call-update) | async-done | bytes 131088 | tf_op jit(solution)/shard_map/reduce_scatter | solution.py:281
  368.2 2.4 convolution_convert_fusion.3
  370.7 9.1 %reduce-scatter.11.cloned.1.call-done = bf16[2,64,512]{2,1,0:T(8,128)(2,1)} async-done(((bf16[2,128,512]{2,1,0:T(8,128)(2,1)}), bf16[2,64,512]{2,1,0:T(8,128)(2,1)}) %reduce-scatter.11.cloned.1.call-update) | async-done | bytes 131088 | tf_op jit(solution)/shard_map/reduce_scatter | solution.py:275
  381.6 1.5 convolution_convert_fusion.4
  383.2 2.1 convolution_convert_fusion.1
  387.5 2.1 convolution_convert_fusion.2
  389.8 4.7 convolution_convert_fusion.5
  394.5 3.8 convolution_convert_fusion.6
  398.4 3.8 convolution_convert_fusion.7
  403.1 1.9 reduce-scatter.17.cloned.1.call-done
  405.0 13.6 %reduce-scatter.21.cloned.1.call-done = bf16[512,1024]{1,0:T(8,128)(2,1)} async-done(((bf16[1024,1024]{1,0:T(8,128)(2,1)}), bf16[512,1024]{1,0:T(8,128)(2,1)}) %reduce-scatter.21.cloned.1.call-update) | async-done | bytes 1048592 | tf_op jit(solution)/shard_map/reduce_scatter | solution.py:322
  418.6 13.6 %reduce-scatter.15.cloned.1.call-done = bf16[512,1024]{1,0:T(8,128)(2,1)} async-done(((bf16[1024,1024]{1,0:T(8,128)(2,1)}), bf16[512,1024]{1,0:T(8,128)(2,1)}) %reduce-scatter.15.cloned.1.call-update) | async-done | bytes 1048592 | tf_op jit(solution)/shard_map/reduce_scatter | solution.py:313
  433.5 11.3 %reduce-scatter.29.cloned.1.call-done = bf16[256,1024]{1,0:T(8,128)(2,1)} async-done(((bf16[512,1024]{1,0:T(8,128)(2,1)}), bf16[256,1024]{1,0:T(8,128)(2,1)}) %reduce-scatter.29.cloned.1.call-update) | async-done | bytes 524304 | tf_op jit(solution)/shard_map/reduce_scatter | solution.py:351
  444.8 2.1 bitcast_convert_fusion
  446.9 10.3 %reduce-scatter.27.cloned.1.call-done = bf16[512,512]{1,0:T(8,128)(2,1)} async-done(((bf16[1024,512]{1,0:T(8,128)(2,1)}), bf16[512,512]{1,0:T(8,128)(2,1)}) %reduce-scatter.27.cloned.1.call-update) | async-done | bytes 524304 | tf_op jit(solution)/shard_map/reduce_scatter | solution.py:348
  457.3 2.1 bitcast_convert_fusion.1
  459.4 10.4 %reduce-scatter.25.cloned.1.call-done = bf16[512,512]{1,0:T(8,128)(2,1)} async-done(((bf16[1024,512]{1,0:T(8,128)(2,1)}), bf16[512,512]{1,0:T(8,128)(2,1)}) %reduce-scatter.25.cloned.1.call-update) | async-done | bytes 524304 | tf_op jit(solution)/shard_map/reduce_scatter | solution.py:345
  469.8 2.2 bitcast_convert_fusion.2
  474.1 2.5 all-reduce.4
  476.7 4.4 reduce-scatter.23.cloned.1.call-done
  481.1 79.0 %all-reduce.2 = (bf16[512]{0:T(512)(128)(2,1)S(1)}, bf16[512,16]{0,1:T(8,128)(2,1)S(1)}, bf16[512]{0:T(512)(128)(2,1)S(1)}) all-reduce(bf16[512]{0:T(512)(128)(2,1)S(1)} %dynamic-slice.1, bf16[512,16]{0,1:T(8,128)(2,1)} %reduce-scatter.23.cloned.1.call-done, ...), channel_id=1, replica_groups=mesh['expert'=16,'shard'=2] {'expert'}, use_global_device_ids=true, to_apply=%region_28.29 | all-reduce | flops 9216 | bytes 36864 | tf_op jit(solution)/shard_map/psum | solution.py:341
  562.8 75.3 %all-reduce.7.cloned.1.call-done = (bf16[512,1024]{1,0:T(8,128)(2,1)}, bf16[512,512]{1,0:T(8,128)(2,1)}, bf16[512,512]{1,0:T(8,128)(2,1)}, bf16[512,1024]{1,0:T(8,128)(2,1)}) async-done(((bf16[512,1024]{1,0:T(8,128)(2,1)}, bf16[512,512]{1,0:T(8,128)(2,1)}, bf16[512,512]{1,0:T(8,128)(2,1)}, bf16[512,1024]{1,0:T(8,128)(2,1)}), (bf16[512,1024]{1,0:T(8,128)(2,1)}, bf16[512,512]{1,0:T(8,128)(2,1)}, ...) | async-done | bytes 3145744 | tf_op jit(solution)/shard_map/psum | solution.py:336
  638.1 2.9 convert_element_type.268
  643.2 1.6 convert_element_type.274
  (279 shorter events, 41.7 us)
Async XLA Ops:
  7.2 181.7 %copy-start = (bf16[1,512,1024]{2,1,0:T(8,128)(2,1)S(1)}, bf16[1,512,1024]{2,1,0:T(8,128)(2,1)}, u32[]{:S(2)}) copy-start(bf16[1,512,1024]{2,1,0:T(8,128)(2,1)} %param.26) | copy-start | bytes 3145732
  7.2 9.7 %copy-start.68 = (s32[2]{0:T(128)S(1)}, s32[2]{0:T(128)}, u32[]{:S(2)}) copy-start(s32[2]{0:T(128)} %constant.65) | copy-start | bytes 28
  7.2 9.8 %copy-start.67 = (s32[2]{0:T(128)S(1)}, s32[2]{0:T(128)}, u32[]{:S(2)}) copy-start(s32[2]{0:T(128)} %constant.62) | copy-start | bytes 28
  7.2 3.3 copy-start.4
  7.2 3.9 copy-start.64
  7.3 14.2 %copy-start.43 = (f32[1024]{0:T(1024)S(1)}, f32[1024]{0:T(1024)}, u32[]{:S(2)}) copy-start(f32[1024]{0:T(1024)} %param.17) | copy-start | bytes 12292
  7.3 14.2 %all-gather.5.cloned.1.call-start = ((), (), s32[]{:S(2)}) async-start(), calls=%async_computation.14 | async-start | bytes 1572864 | tf_op jit(solution)/shard_map/all_gather | solution.py:80
  8.0 25.2 %all-gather.7.cloned.1.call-start = ((), (), s32[]{:S(2)}) async-start(), calls=%async_computation.15 | async-start | bytes 1572864 | tf_op jit(solution)/shard_map/all_gather | solution.py:79
  8.7 37.8 %all-gather.9.cloned.1.call-start = ((), (), s32[]{:S(2)}) async-start(), calls=%async_computation.16 | async-start | bytes 3145728 | tf_op jit(solution)/shard_map/all_gather | solution.py:78
  9.5 50.2 %all-gather.11.cloned.1.call-start = ((), (), s32[]{:S(2)}) async-start(), calls=%async_computation.17 | async-start | bytes 3145728 | tf_op jit(solution)/shard_map/all_gather | solution.py:81
  11.2 35.4 %copy-start.54 = (f32[128]{0:T(128)}, f32[128]{0:T(128)S(1)}, u32[]{:S(2)}) copy-start(f32[128]{0:T(128)S(1)} %fusion.57) | copy-start | bytes 1540
  17.8 31.3 %copy-start.39 = (f32[128,32]{0,1:T(8,128)}, f32[128,32]{0,1:T(8,128)S(1)}, u32[]{:S(2)}) copy-start(f32[128,32]{0,1:T(8,128)S(1)} %get-tuple-element.49) | copy-start | bytes 49156
  25.2 25.6 %copy-start.34 = (bf16[2,128,512]{1,2,0:T(8,128)(2,1)}, bf16[2,128,512]{1,2,0:T(8,128)(2,1)S(1)}, u32[]{:S(2)}) copy-start(bf16[2,128,512]{1,2,0:T(8,128)(2,1)S(1)} %copy.143) | copy-start | bytes 786436
  37.6 11.9 %copy-start.16 = (bf16[2,128,512]{1,2,0:T(8,128)(2,1)}, bf16[2,128,512]{1,2,0:T(8,128)(2,1)S(1)}, u32[]{:S(2)}) copy-start(bf16[2,128,512]{1,2,0:T(8,128)(2,1)S(1)} %copy.149) | copy-start | bytes 786436
  53.0 9.7 %copy-start.50 = (f32[1024]{0:T(1024)S(1)}, f32[1024]{0:T(1024)}, u32[]{:S(2)}) copy-start(f32[1024]{0:T(1024)} %param.23) | copy-start | bytes 12292
  53.4 8.6 %copy-start.18 = (bf16[128,1024]{1,0:T(8,128)(2,1)}, bf16[128,1024]{1,0:T(8,128)(2,1)S(1)}, u32[]{:S(2)}) copy-start(bf16[128,1024]{1,0:T(8,128)(2,1)S(1)} %convert_element_type.235) | copy-start | bytes 786436
  61.9 10.6 %copy-start.62 = (f32[128]{0:T(128)}, f32[128]{0:T(128)S(1)}, u32[]{:S(2)}) copy-start(f32[128]{0:T(128)S(1)} %fusion.58) | copy-start | bytes 1540
  72.5 7.0 %copy-start.56 = (bf16[512,16]{0,1:T(8,128)(2,1)S(1)}, bf16[512,16]{0,1:T(8,128)(2,1)}, u32[]{:S(2)}) copy-start(bf16[512,16]{0,1:T(8,128)(2,1)} %param.22) | copy-start | bytes 49156
  72.5 9.1 %copy-start.32 = (bf16[128,1024]{1,0:T(8,128)(2,1)S(1)}, bf16[128,1024]{1,0:T(8,128)(2,1)}, u32[]{:S(2)}) copy-start(bf16[128,1024]{1,0:T(8,128)(2,1)} %param.27) | copy-start | bytes 786436
  72.5 10.0 %copy-start.14 = (bf16[128,1024]{1,0:T(8,128)(2,1)S(1)}, bf16[128,1024]{1,0:T(8,128)(2,1)}, u32[]{:S(2)}) copy-start(bf16[128,1024]{1,0:T(8,128)(2,1)} %multiply_convert_fusion.5) | copy-start | bytes 786436
  72.5 10.1 %copy-start.52 = (s32[128,8]{0,1:T(8,128)S(1)}, s32[128,8]{0,1:T(8,128)}, u32[]{:S(2)}) copy-start(s32[128,8]{0,1:T(8,128)} %param.16) | copy-start | bytes 12292
  72.5 54.7 %all-to-all-start = ((bf16[16,68,1024]{2,1,0:T(8,128)(2,1)}), bf16[16,68,1024]{2,1,0:T(8,128)(2,1)}, u32[]{:S(2)}, u32[]{:S(2)}) async-start(bf16[16,68,1024]{2,1,0:T(8,128)(2,1)} %copy.159), calls=%async_computation | async-start | bytes 4718592 | tf_op jit(solution)/shard_map/all_to_all | solution.py:159
  127.2 59.1 %all-to-all-start.2 = ((bf16[16,68,1024]{2,1,0:T(8,128)(2,1)}), bf16[16,68,1024]{2,1,0:T(8,128)(2,1)}, u32[]{:S(2)}, u32[]{:S(2)}) async-start(bf16[16,68,1024]{2,1,0:T(8,128)(2,1)} %copy.162), calls=%async_computation.2 | async-start | bytes 4718592 | tf_op jit(solution)/shard_map/all_to_all | solution.py:200
  141.7 4.9 copy-start.20
  141.7 4.9 copy-start.71
  188.9 6.8 %copy-start.22 = (bf16[1088,1024]{1,0:T(8,128)(2,1)}, bf16[1088,1024]{1,0:T(8,128)(2,1)S(1)}, u32[]{:S(2)}) copy-start(bf16[1088,1024]{1,0:T(8,128)(2,1)S(1)} %reshape.441) | copy-start | bytes 6684676
  200.2 20.6 %copy-start.72 = (bf16[1,1024,512]{2,1,0:T(8,128)(2,1)S(1)}, bf16[1,1024,512]{2,1,0:T(8,128)(2,1)}, u32[]{:S(2)}) copy-start(bf16[1,1024,512]{2,1,0:T(8,128)(2,1)} %param.24) | copy-start | bytes 3145732
  200.2 20.6 %copy-start.74 = (bf16[1088,512]{1,0:T(8,128)(2,1)S(1)}, bf16[1088,512]{1,0:T(8,128)(2,1)}, u32[]{:S(2)}) copy-start(bf16[1088,512]{1,0:T(8,128)(2,1)} %get-tuple-element.30) | copy-start | bytes 3342340
  200.2 67.6 %all-to-all-start.1 = ((bf16[16,68,1024]{2,1,0:T(8,128)(2,1)}), bf16[16,68,1024]{2,1,0:T(8,128)(2,1)}, u32[]{:S(2)}, u32[]{:S(2)}) async-start(bf16[16,68,1024]{2,1,0:T(8,128)(2,1)} %reshape.440), calls=%async_computation.1 | async-start | bytes 4718592 | tf_op jit(solution)/shard_map/all_to_all | solution.py:167
  225.9 52.7 %copy-start.46 = (f32[2,8,2,64]{3,2,1,0:T(2,128)S(1)}, f32[2,8,2,64]{3,2,1,0:T(2,128)}, u32[]{:S(2)}) copy-start(f32[2,8,2,64]{3,2,1,0:T(2,128)} %copy-done.45) | copy-start | bytes 24580
  225.9 52.7 %copy-start.49 = (f32[2,8,2,64]{3,2,1,0:T(2,128)S(1)}, f32[2,8,2,64]{3,2,1,0:T(2,128)}, u32[]{:S(2)}) copy-start(f32[2,8,2,64]{3,2,1,0:T(2,128)} %copy-done.48) | copy-start | bytes 24580
  267.9 57.8 %all-to-all-start.3 = ((bf16[16,68,1024]{2,1,0:T(8,128)(2,1)}), bf16[16,68,1024]{2,1,0:T(8,128)(2,1)}, u32[]{:S(2)}, u32[]{:S(2)}) async-start(bf16[16,68,1024]{2,1,0:T(8,128)(2,1)} %reshape.442), calls=%async_computation.3 | async-start | bytes 4718592 | tf_op jit(solution)/shard_map/all_to_all | solution.py:224
  278.5 89.7 %reduce-scatter.13.cloned.1.call-start = ((), (), s32[]{:S(2)}) async-start(), calls=%async_computation.19 | async-start | bytes 393216 | tf_op jit(solution)/shard_map/reduce_scatter | solution.py:281
  282.1 15.2 %copy-start.11 = (f32[128,1024]{1,0:T(8,128)S(1)}, f32[128,1024]{1,0:T(8,128)}, u32[]{:S(2)}) copy-start(f32[128,1024]{1,0:T(8,128)} %convert_multiply_fusion.6) | copy-start | bytes 1572868
  297.3 3.3 copy-start.58
  297.3 3.3 copy-start.61
  297.3 3.4 copy-start.53
  343.7 3.1 copy-start.42
  343.7 3.1 copy-start.63
  343.7 4.0 copy-start.70
  343.7 4.0 copy-start.33
  348.7 34.5 %copy-start.7 = (f32[128,1024]{1,0:T(8,128)}, f32[128,1024]{1,0:T(8,128)S(1)}, u32[]{:S(2)}) copy-start(f32[128,1024]{1,0:T(8,128)S(1)} %get-tuple-element.38) | copy-start | bytes 1572868
  355.4 24.4 %reduce-scatter.11.cloned.1.call-start = ((), (), s32[]{:S(2)}) async-start(), calls=%async_computation.18 | async-start | bytes 393216 | tf_op jit(solution)/shard_map/reduce_scatter | solution.py:275
  355.7 12.5 %copy-start.55 = (f32[128]{0:T(128)S(1)}, f32[128]{0:T(128)}, u32[]{:S(2)}) copy-start(f32[128]{0:T(128)} %copy-done.54) | copy-start | bytes 1540
  358.1 45.0 %reduce-scatter.19.cloned.1.call-start = ((), (), s32[]{:S(2)}) async-start(), calls=%async_computation.22 | async-start | bytes 1572864 | tf_op jit(solution)/shard_map/reduce_scatter | solution.py:319
  370.6 10.9 %copy-start.40 = (f32[128,32]{0,1:T(8,128)S(1)}, f32[128,32]{0,1:T(8,128)}, u32[]{:S(2)}) copy-start(f32[128,32]{0,1:T(8,128)} %copy-done.39) | copy-start | bytes 49156
  370.7 10.9 %copy-start.47 = (f32[128,32]{0,1:T(8,128)S(1)}, f32[128,32]{0,1:T(8,128)}, u32[]{:S(2)}) copy-start(f32[128,32]{0,1:T(8,128)} %get-tuple-element.47) | copy-start | bytes 49156
  370.7 34.3 %reduce-scatter.17.cloned.1.call-start = ((), (), s32[]{:S(2)}) async-start(), calls=%async_computation.21 | async-start | bytes 1572864 | tf_op jit(solution)/shard_map/reduce_scatter | solution.py:316
  381.6 3.7 copy-start.27
  383.2 35.5 %reduce-scatter.21.cloned.1.call-start = ((), (), s32[]{:S(2)}) async-start(), calls=%async_computation.23 | async-start | bytes 3145728 | tf_op jit(solution)/shard_map/reduce_scatter | solution.py:322
  385.3 46.9 %reduce-scatter.15.cloned.1.call-start = ((), (), s32[]{:S(2)}) async-start(), calls=%async_computation.20 | async-start | bytes 3145728 | tf_op jit(solution)/shard_map/reduce_scatter | solution.py:313
  389.7 4.8 copy-start.21
  389.7 55.1 %reduce-scatter.29.cloned.1.call-start = ((), (), s32[]{:S(2)}) async-start(), calls=%async_computation.27 | async-start | bytes 1572864 | tf_op jit(solution)/shard_map/reduce_scatter | solution.py:351
  394.4 62.8 %reduce-scatter.27.cloned.1.call-start = ((), (), s32[]{:S(2)}) async-start(), calls=%async_computation.26 | async-start | bytes 1572864 | tf_op jit(solution)/shard_map/reduce_scatter | solution.py:348
  398.3 3.9 copy-start.15
  398.3 71.5 %reduce-scatter.25.cloned.1.call-start = ((), (), s32[]{:S(2)}) async-start(), calls=%async_computation.25 | async-start | bytes 1572864 | tf_op jit(solution)/shard_map/reduce_scatter | solution.py:345
  402.2 30.1 %copy-start.73 = (u32[32]{0:T(128)S(1)}, u32[32]{0:T(128)}, u32[]{:S(2)}) copy-start(u32[32]{0:T(128)} %constant.105) | copy-start | bytes 388
  402.2 78.9 %reduce-scatter.23.cloned.1.call-start = ((), (), s32[]{:S(2)}) async-start(), calls=%async_computation.24 | async-start | bytes 49152 | tf_op jit(solution)/shard_map/reduce_scatter | solution.py:325
  403.0 235.1 %all-reduce.7.cloned.1.call-start = ((), (), s32[]{:S(2)}) async-start(), calls=%async_computation.28 | async-start | bytes 6291456 | tf_op jit(solution)/shard_map/psum | solution.py:336
  433.5 38.6 %copy-start.5 = (bf16[1024,1024]{1,0:T(8,128)(2,1)S(1)}, bf16[1024,1024]{1,0:T(8,128)(2,1)}, u32[]{:S(2)}) copy-start(bf16[1024,1024]{1,0:T(8,128)(2,1)} %all-gather.9.cloned.1.call-done) | copy-start | bytes 6291460
  459.4 13.5 %copy-start.28 = (bf16[128,8,64]{0,2,1:T(8,128)(2,1)S(1)}, bf16[128,8,64]{0,2,1:T(8,128)(2,1)}, u32[]{:S(2)}) copy-start(bf16[128,8,64]{0,2,1:T(8,128)(2,1)} %copy-done.27) | copy-start | bytes 393220
  472.9 88.9 %copy-start.66 = (f32[128]{0:T(128)S(1)}, f32[128]{0:T(128)}, u32[]{:S(2)}) copy-start(f32[128]{0:T(128)} %copy-done.65) | copy-start | bytes 1540
  472.9 88.9 %copy-start.8 = (f32[128,1024]{1,0:T(8,128)S(1)}, f32[128,1024]{1,0:T(8,128)}, u32[]{:S(2)}) copy-start(f32[128,1024]{1,0:T(8,128)} %copy-done.7) | copy-start | bytes 1572868
  638.1 4.0 copy-start.36
  (31 other events, 51.0 us)
Sparse Core Ops, SparseCore 0:
  9.6 11.7 all-gather.4
  23.0 10.1 all-gather.6
  34.8 11.7 all-gather.8
  47.9 11.7 all-gather.10
  355.5 12.6 reduce-scatter.12
  371.0 8.8 reduce-scatter.10
  382.6 9.6 reduce-scatter.18
  395.3 9.6 reduce-scatter.16
  407.8 10.7 reduce-scatter.20
  421.4 10.7 reduce-scatter.14
  435.0 9.7 reduce-scatter.28
  447.5 9.6 reduce-scatter.26
  460.1 9.6 reduce-scatter.24
  472.5 8.5 reduce-scatter.22
  488.1 150.0 all-reduce.6
where the time goes:
time: 661 us; the launch traced here: 652 us
  waiting for transfers between devices  325 us (49%)
  blocking collectives  87.5 us (13%)
  local copies, waits for them, and re-layouts  73.7 us (11%)
  matrix products  57 us (9%)
  starting transfers between devices  50.9 us (8%)
  other arithmetic  41.2 us (6%)
  between operations  16.1 us (2%)
    psum x1, blocking collectives, on_device(): lax.psum(shard_sums[5].astype(jnp.bfloat16), 'expert').astype(jnp.float32)  79 us
    psum x1, waiting for transfers between devices, on_device(): lax.psum(shard_sums[0].astype(jnp.bfloat16), 'expert').astype(jnp.float32)  75.3 us
    all_to_all x1, waiting for transfers between devices, on_device(): lax.all_to_all(result.reshape(source_count, slot_count, model_width), 'ex...  42 us
    all_to_all x1, waiting for transfers between devices, on_device(): lax.all_to_all(send_grads, 'expert', split_axis=0, concat_axis=0, tiled=T...  37 us
    all_to_all x1, waiting for transfers between devices, on_device(): lax.all_to_all(send_rows, 'expert', split_axis=0, concat_axis=0, tiled=True)  32.3 us
    all_to_all x1, waiting for transfers between devices, on_device(): lax.all_to_all(row_grads.reshape(expert_count, capacity, model_width), 'e...  24.9 us
    all_to_all x1, starting transfers between devices, on_device(): lax.all_to_all(result.reshape(source_count, slot_count, model_width), 'ex...  20.6 us
    gather x1, local copies, waits for them, and re-layouts, on_device(): returned[slot_expert, slot_place].reshape(tok_count, TOP, model_width)  15.2 us
  transfers between devices with their start and end apart: 19, of which 18 were waited for; matrix products, arithmetic and copies ran while one was open for 16% of the time, Pallas kernels for 0%

commit v1 on v0

v1 whole, which is shorter than its diff:
```python
import functools

import jax
import jax.numpy as jnp
from jax import lax
from jax.experimental import pallas as pl
from jax.experimental.pallas import tpu as pltpu
from jax.sharding import PartitionSpec as P

HEADS = 16
KV_HEADS = 8
HEAD_DIM = 64
TOP = 8


epsilon = 1e-06
res_scale = 0.22
att_scale = 0.015625
rope_base = 10000.0
masked_score = -1e30


def rms_norm(values, gain):
    return values * lax.rsqrt(jnp.mean(values * values, -1, keepdims=True) + epsilon) * gain


def doc_layout(lengths, positions):
    doc_ends = jnp.cumsum(lengths)
    past_end = positions[:, None] >= doc_ends[None, :]
    doc_index = jnp.sum(past_end.astype(jnp.int32), 1)
    doc_start = jnp.sum(jnp.where(past_end, lengths[None, :], 0), 1)
    return (doc_index, positions - doc_start)


def rope_tables(offsets):
    half_size = HEAD_DIM // 2
    frequency = rope_base ** (-2.0 * jnp.arange(half_size).astype(jnp.float32) / HEAD_DIM)
    angles = offsets.astype(jnp.float32)[:, None] * frequency[None, :]
    return (jnp.cos(angles), jnp.sin(angles))


def rotate(values, cos_table, sin_table, inverse):
    row_count = values.shape[0]
    shaped = values.reshape(row_count, -1, HEAD_DIM)
    half_size = HEAD_DIM // 2
    front_part = shaped[:, :, :half_size]
    back_part = shaped[:, :, half_size:]
    cos_wide = cos_table[:, None, :]
    sin_wide = sin_table[:, None, :]
    if inverse:
        sin_wide = -sin_wide
    turned = jnp.concatenate(
        [
            front_part * cos_wide - back_part * sin_wide,
            back_part * cos_wide + front_part * sin_wide,
        ],
        -1,
    )
    return turned.reshape(row_count, -1)


MESH_ID = pl.DeviceIdType.MESH
vmem_grant = 48 * 1024 * 1024


def greet(devices):
    barrier = pltpu.get_barrier_semaphore()
    for device in devices:
        pl.semaphore_signal(barrier, inc=1, device_id=device, device_id_type=MESH_ID)
    pl.semaphore_wait(barrier, len(devices))


def gather_kernel(count, *refs):
    sources, results = refs[:count], refs[count : 2 * count]
    send_sem, recv_sem, own_sem = refs[2 * count :]
    expert_index, shard_index = lax.axis_index("expert"), lax.axis_index("shard")
    other = (expert_index, 1 - shard_index)
    greet([other])
    copies = []
    for at in range(count):
        copies.append(
            pltpu.make_async_remote_copy(
                src_ref=sources[at],
                dst_ref=results[at].at[shard_index],
                send_sem=send_sem.at[at],
                recv_sem=recv_sem.at[at],
                device_id=other,
                device_id_type=MESH_ID,
            )
        )
        copies.append(
            pltpu.make_async_copy(sources[at], results[at].at[shard_index], own_sem.at[at])
        )
    for copy in copies:
        copy.start()
    for copy in copies:
        copy.wait()


def gather_pair(arrays, identity):
    count = len(arrays)
    return pl.pallas_call(
        functools.partial(gather_kernel, count),
        out_shape=[jax.ShapeDtypeStruct((2,) + a.shape, a.dtype) for a in arrays],
        in_specs=[pl.BlockSpec(memory_space=pl.ANY)] * count,
        out_specs=[pl.BlockSpec(memory_space=pl.ANY)] * count,
        scratch_shapes=[pltpu.SemaphoreType.DMA((count,))] * 3,
        compiler_params=pltpu.CompilerParams(collective_id=identity, has_side_effects=True),
    )(*arrays)


def swap_kernel(source, result, send_sem, recv_sem):
    expert_index, shard_index = lax.axis_index("expert"), lax.axis_index("shard")
    other = (expert_index, 1 - shard_index)
    greet([other])
    copy = pltpu.make_async_remote_copy(
        src_ref=source.at[1 - shard_index],
        dst_ref=result,
        send_sem=send_sem,
        recv_sem=recv_sem,
        device_id=other,
        device_id_type=MESH_ID,
    )
    copy.start()
    copy.wait()


def swap_pair(array, identity):
    return pl.pallas_call(
        swap_kernel,
        out_shape=jax.ShapeDtypeStruct(array.shape[1:], array.dtype),
        in_specs=[pl.BlockSpec(memory_space=pl.ANY)],
        out_specs=pl.BlockSpec(memory_space=pl.ANY),
        scratch_shapes=[pltpu.SemaphoreType.DMA, pltpu.SemaphoreType.DMA],
        compiler_params=pltpu.CompilerParams(collective_id=identity, has_side_effects=True),
    )(array)


def add_rows(target, target_at, first, first_at, second, second_at, rows):
    step = min(rows, 32)

    def one(index, carry):
        row = index * step
        into = pl.ds(pl.multiple_of(target_at + row, step), step)
        left = pl.ds(pl.multiple_of(first_at + row, step), step)
        right = pl.ds(pl.multiple_of(second_at + row, step), step)
        total = first[left, :].astype(jnp.float32) + second[right, :].astype(jnp.float32)
        target[into, :] = total.astype(target.dtype)
        return carry

    lax.fori_loop(0, rows // step, one, 0)


def reduce_kernel(levels, parts, swaps, *refs):
    refs = list(refs)

    def take(amount):
        taken = refs[:amount]
        del refs[:amount]
        return taken

    sources, swap_sources = take(parts), take(swaps)
    totals, swap_results = take(parts), take(swaps)
    near, far, held_sums = take(parts), take(parts), take(parts)
    send_sem, recv_sem, swap_send, swap_recv = refs
    expert_index, shard_index = lax.axis_index("expert"), lax.axis_index("shard")
    other = (expert_index, 1 - shard_index)
    held = [(expert_index // (1 << bit)) % 2 for bit in range(levels)]
    partners = [
        (expert_index + (1 << bit) * (1 - 2 * held[bit]), shard_index) for bit in range(levels)
    ]
    greet([other] + partners)
    rows = totals[0].shape[0]

    def send(part, step, source, target, device):
        copy = pltpu.make_async_remote_copy(
            src_ref=source,
            dst_ref=target,
            send_sem=send_sem.at[part, step],
            recv_sem=recv_sem.at[part, step],
            device_id=device,
            device_id_type=MESH_ID,
        )
        copy.start()
        return copy

    flying = []
    for part in range(parts):
        away = pl.ds(pl.multiple_of((1 - shard_index) * rows, rows), rows)
        flying.append(send(part, 0, sources[part].at[away], near[part], other))
    swapping = []
    for at in range(swaps):
        copy = pltpu.make_async_remote_copy(
            src_ref=swap_sources[at].at[1 - shard_index],
            dst_ref=swap_results[at],
            send_sem=swap_send.at[at],
            recv_sem=swap_recv.at[at],
            device_id=other,
            device_id_type=MESH_ID,
        )
        copy.start()
        swapping.append(copy)
    starts = [0] * parts
    size = rows
    landing = 0
    for step in range(2 * levels + 1):
        for part in range(parts):
            flying[part].wait()
            if step == 0:
                add_rows(
                    held_sums[part], 0, sources[part], shard_index * rows, near[part], 0, rows
                )
            elif step <= levels:
                bit = (step - 1 + part) % levels
                starts[part] = starts[part] + held[bit] * (size // 2)
                add_rows(
                    totals[part] if step == levels else held_sums[part],
                    starts[part],
                    held_sums[part],
                    starts[part],
                    far[part],
                    landing,
                    size // 2,
                )
            else:
                bit = (2 * levels - step + part) % levels
                starts[part] = starts[part] - held[bit] * size
            if step < levels:
                half = (size if step == 0 else size // 2) // 2
                bit = (step + part) % levels
                leaving = pl.multiple_of(starts[part] + (1 - held[bit]) * half, half)
                room = 0 if step == 0 else landing + size // 2
                flying[part] = send(
                    part,
                    step + 1,
                    held_sums[part].at[pl.ds(leaving, half)],
                    far[part].at[pl.ds(room, half)],
                    partners[bit],
                )
            elif step < 2 * levels:
                whole = size // 2 if step == levels else size * 2
                bit = (2 * levels - 1 - step + part) % levels
                region = pl.ds(pl.multiple_of(starts[part], whole), whole)
                flying[part] = send(
                    part, step + 1, totals[part].at[region], totals[part].at[region], partners[bit]
                )
        if 1 <= step <= levels:
            landing += size // 2
            size //= 2
        elif step > levels:
            size *= 2
    for copy in swapping:
        copy.wait()


def reduce_all(sources, swap_sources, expert_count, identity):
    parts, swaps = len(sources), len(swap_sources)
    levels = expert_count.bit_length() - 1
    rows = sources[0].shape[0] // 2
    spec = pl.BlockSpec(memory_space=pltpu.VMEM)
    return pl.pallas_call(
        functools.partial(reduce_kernel, levels, parts, swaps),
        out_shape=[jax.ShapeDtypeStruct((rows, a.shape[1]), a.dtype) for a in sources]
        + [jax.ShapeDtypeStruct(a.shape[1:], a.dtype) for a in swap_sources],
        in_specs=[spec] * (parts + swaps),
        out_specs=[spec] * (parts + swaps),
        scratch_shapes=[pltpu.VMEM((rows, a.shape[1]), a.dtype) for a in list(sources) * 3]
        + [pltpu.SemaphoreType.DMA((parts, 2 * levels + 1))] * 2
        + [pltpu.SemaphoreType.DMA((swaps,))] * 2,
        compiler_params=pltpu.CompilerParams(
            collective_id=identity, has_side_effects=True, vmem_limit_bytes=vmem_grant
        ),
    )(*sources, *swap_sources)


def on_device(
    hidden_in,
    doc_lengths,
    routes,
    attn_norm_gain,
    query_weight,
    key_weight,
    value_weight,
    output_weight,
    router_weight,
    moe_norm_gain,
    gate_weight,
    up_weight,
    down_weight,
    cotangent,
):
    low = jnp.bfloat16
    wide = jnp.float32
    tok_count, model_width = hidden_in.shape
    shard_index = lax.axis_index("shard")
    shard_count = lax.axis_size("shard")
    expert_axis = lax.axis_size("expert")
    expert_index = lax.axis_index("expert")
    paired = shard_count == 2
    expert_count = router_weight.shape[1]
    capacity = 17 * tok_count * TOP // (16 * expert_count)
    capacity = -(-capacity // 8) * 8
    sub_rows = tok_count // 2
    seq_len = sub_rows * shard_count
    group_ratio = HEADS // KV_HEADS
    kv_width = key_weight.shape[1]

    picks = jnp.any(
        routes[:, :, None] == jnp.arange(expert_count, dtype=jnp.int32)[None, None, :], 1
    )
    picks_low = picks.astype(low)
    earlier = jnp.tril(jnp.ones((tok_count, tok_count), low), -1)
    place = jnp.dot(earlier, picks_low, preferred_element_type=wide).astype(jnp.int32)
    place = jnp.where(picks, place, -1)
    hot = (
        place.T[:, None, :] == jnp.arange(capacity, dtype=jnp.int32)[None, :, None]
    ).astype(low)
    hot = hot.reshape(expert_count * capacity, tok_count)

    def to_slots(values):
        rows = jnp.dot(hot, values, preferred_element_type=wide).astype(low)
        return rows.reshape(expert_count, capacity, -1)

    def cross(values):
        return lax.all_to_all(values, "expert", split_axis=0, concat_axis=0, tiled=True)

    picks_wide = jnp.pad(picks_low, ((0, 0), (0, -expert_count % 128)))
    arrived_top = cross(to_slots(jnp.concatenate([cotangent, picks_wide], 1)))

    router_wide = jnp.pad(router_weight, ((0, 0), (0, -expert_count % 128)))
    weights = [query_weight, key_weight, value_weight, output_weight, router_wide]
    if paired:
        gathered = [a.reshape(-1, a.shape[2]) for a in gather_pair(weights, 1)]
    else:
        gathered = [lax.all_gather(a, "shard", axis=0, tiled=True) for a in weights]
    query_full, key_full, value_full, output_full, router_padded = gathered
    router_full = router_padded[:, :expert_count]

    input_float = hidden_in.astype(wide)
    normed_one = rms_norm(input_float, attn_norm_gain).astype(low)
    query_raw = jnp.dot(normed_one, query_full, preferred_element_type=wide)
    key_raw = jnp.dot(normed_one, key_full, preferred_element_type=wide)
    value_raw = jnp.dot(normed_one, value_full, preferred_element_type=wide)
    own_positions = shard_index * sub_rows + jnp.arange(sub_rows, dtype=jnp.int32)
    seq_positions = jnp.arange(seq_len, dtype=jnp.int32)
    layout_both = jax.vmap(doc_layout, in_axes=(0, None))
    query_docs, query_offsets = layout_both(doc_lengths, own_positions)
    key_docs, unused_offsets = layout_both(doc_lengths, seq_positions)
    cos_table, sin_table = rope_tables(query_offsets.reshape(-1))
    query_rot = rotate(query_raw, cos_table, sin_table, False).astype(low)
    key_rot = rotate(key_raw, cos_table, sin_table, False).astype(low)
    value_low = value_raw.astype(low)
    both = jnp.concatenate([key_rot, value_low], 1)
    if paired:
        both_group = gather_pair([both], 2)[0]
    else:
        both_group = lax.all_gather(both, "shard", axis=0)
    both_group = both_group.reshape(shard_count, 2, sub_rows, 2 * kv_width)
    both_group = both_group.transpose(1, 0, 2, 3).reshape(2, seq_len, 2 * kv_width)
    allowed = (
        (own_positions[None, :, None] >= seq_positions[None, None, :])
        & (query_docs[:, :, None] == key_docs[:, None, :])
    )[:, None, None]
    query_heads = query_rot.reshape(2, sub_rows, KV_HEADS, group_ratio, HEAD_DIM)
    key_heads = both_group[:, :, :kv_width].reshape(2, seq_len, KV_HEADS, HEAD_DIM)
    value_heads = both_group[:, :, kv_width:].reshape(2, seq_len, KV_HEADS, HEAD_DIM)
    scores = (
        jnp.einsum("btkgd,bskd->bkgts", query_heads, key_heads, preferred_element_type=wide)
        * att_scale
    )
    scores = jnp.where(allowed, scores, masked_score)
    exp_scores = jnp.exp(scores - jnp.max(scores, -1, keepdims=True))
    probs = exp_scores / jnp.sum(exp_scores, -1, keepdims=True)
    probs_low = probs.astype(low)
    attn_mix = jnp.einsum("bkgts,bskd->btkgd", probs_low, value_heads, preferred_element_type=wide)
    attn_low = attn_mix.reshape(tok_count, -1).astype(low)
    branch = jnp.dot(attn_low, output_full, preferred_element_type=wide)
    middle = input_float + res_scale * branch
    normed_two = rms_norm(middle, moe_norm_gain).astype(low)
    arrived = cross(to_slots(normed_two))

    def gate_softmax(rows, chosen):
        logits = jnp.dot(rows, router_full, preferred_element_type=wide)
        top = jnp.max(jnp.where(chosen, logits, -jnp.inf), -1, keepdims=True)
        top = jnp.where(jnp.any(chosen, -1, keepdims=True), top, 0.0)
        powers = jnp.where(chosen, jnp.exp(jnp.where(chosen, logits - top, 0.0)), 0.0)
        total = jnp.sum(powers, -1, keepdims=True)
        return powers / jnp.where(total > 0.0, total, 1.0)

    gates = gate_softmax(normed_two, picks)

    gate_matrix = gate_weight[0]
    up_matrix = up_weight[0]
    down_matrix = down_weight[0]
    flat_rows = arrived.reshape(-1, model_width)
    gate_pre = jnp.dot(flat_rows, gate_matrix, preferred_element_type=wide)
    up_pre = jnp.dot(flat_rows, up_matrix, preferred_element_type=wide)
    sigmoid_gate = jax.nn.sigmoid(gate_pre)
    activated = gate_pre * sigmoid_gate
    inner = (activated * up_pre).astype(low)
    result = jnp.dot(inner, down_matrix, preferred_element_type=wide).astype(low)
    returned = cross(result.reshape(expert_axis, -1, model_width)).reshape(-1, model_width)

    flat_top = arrived_top.reshape(-1, arrived_top.shape[2])
    slot_picks = flat_top[:, model_width : model_width + expert_count] > 0.5
    slot_gates = gate_softmax(flat_rows, slot_picks)
    mine = jnp.arange(expert_count, dtype=jnp.int32)[None, :] == expert_index
    own_gate = jnp.sum(jnp.where(mine, slot_gates, 0.0), 1, keepdims=True)
    flat_grads = (own_gate * (res_scale * flat_top[:, :model_width].astype(wide))).astype(low)
    inner_grad = jnp.einsum("rd,fd->rf", flat_grads, down_matrix, preferred_element_type=wide)
    gate_pregrad = (
        inner_grad * up_pre * sigmoid_gate * (1.0 + gate_pre * (1.0 - sigmoid_gate))
    ).astype(low)
    up_pregrad = (inner_grad * activated).astype(low)
    row_grads = (
        jnp.einsum("rf,df->rd", gate_pregrad, gate_matrix, preferred_element_type=wide)
        + jnp.einsum("rf,df->rd", up_pregrad, up_matrix, preferred_element_type=wide)
    ).astype(low)
    back_grads = cross(row_grads.reshape(expert_axis, -1, model_width)).reshape(-1, model_width)
    down_wgrad = jnp.einsum("rf,rd->fd", inner, flat_grads, preferred_element_type=wide).astype(low)
    gate_wgrad = jnp.einsum(
        "rd,rf->df", flat_rows, gate_pregrad, preferred_element_type=wide
    ).astype(low)
    up_wgrad = jnp.einsum(
        "rd,rf->df", flat_rows, up_pregrad, preferred_element_type=wide
    ).astype(low)

    gates_slots = jnp.repeat(gates.T, capacity, 0) * hot.astype(wide)
    gates_high = gates_slots.astype(low)
    gates_rest = (gates_slots - gates_high.astype(wide)).astype(low)
    mixture = jnp.einsum(
        "rt,rd->td", gates_high, returned, preferred_element_type=wide
    ) + jnp.einsum("rt,rd->td", gates_rest, returned, preferred_element_type=wide)
    layer_out = (middle + res_scale * mixture).astype(low)
    grad_out = cotangent.astype(wide)
    all_dots = jnp.einsum("rd,td->rt", returned, cotangent, preferred_element_type=wide)
    grad_gates = (
        res_scale
        * jnp.sum(
            (all_dots * hot.astype(wide)).reshape(expert_count, capacity, tok_count), 1
        ).T
    )
    gate_dot = jnp.sum(gates * grad_gates, 1, keepdims=True)
    logit_grad = (gates * (grad_gates - gate_dot)).astype(low)
    router_wgrad = jnp.einsum("td,te->de", normed_two, logit_grad, preferred_element_type=wide)
    router_back = jnp.einsum("te,de->td", logit_grad, router_full, preferred_element_type=wide)
    (
        back_grads,
        layer_out,
        router_back,
        router_wgrad,
        down_wgrad,
        gate_wgrad,
        up_wgrad,
    ) = lax.optimization_barrier(
        (back_grads, layer_out, router_back, router_wgrad, down_wgrad, gate_wgrad, up_wgrad)
    )
    normed_two_grad = (
        jnp.einsum("rt,rd->td", hot, back_grads, preferred_element_type=wide) + router_back
    )
    unused_value, second_pull = jax.vjp(rms_norm, middle, moe_norm_gain)
    middle_from_norm, moe_gain_grad = second_pull(normed_two_grad)
    middle_grad = grad_out + middle_from_norm
    branch_grad = (res_scale * middle_grad).astype(low)
    output_wgrad = jnp.einsum("tq,td->qd", attn_low, branch_grad, preferred_element_type=wide)
    attn_grad = jnp.einsum(
        "td,qd->tq", branch_grad, output_full, preferred_element_type=wide
    ).astype(low)
    attn_grad = attn_grad.reshape(2, sub_rows, KV_HEADS, group_ratio, HEAD_DIM)
    prob_grad = jnp.einsum("btkgd,bskd->bkgts", attn_grad, value_heads, preferred_element_type=wide)
    value_part = jnp.einsum("bkgts,btkgd->bskd", probs_low, attn_grad, preferred_element_type=wide)
    score_grad = (probs * (prob_grad - jnp.sum(probs * prob_grad, -1, keepdims=True))).astype(low)
    query_rot_grad = att_scale * jnp.einsum(
        "bkgts,bskd->btkgd", score_grad, key_heads, preferred_element_type=wide
    )
    key_part = att_scale * jnp.einsum(
        "bkgts,btkgd->bskd", score_grad, query_heads, preferred_element_type=wide
    )
    both_part = jnp.concatenate(
        [key_part.reshape(2, seq_len, -1), value_part.reshape(2, seq_len, -1)], -1
    ).astype(low)
    both_part = both_part.reshape(2, shard_count, sub_rows, 2 * kv_width).transpose(1, 0, 2, 3)
    both_part = both_part.reshape(shard_count, tok_count, 2 * kv_width)

    def own_block(values):
        return lax.dynamic_index_in_dim(values, shard_index, 0, keepdims=False).astype(wide)

    if paired:
        both_pre = own_block(both_part) + swap_pair(both_part, 3).astype(wide)
    else:
        both_pre = lax.psum_scatter(both_part, "shard", scatter_dimension=0).astype(wide)
    query_pre_grad = rotate(
        query_rot_grad.reshape(tok_count, -1), cos_table, sin_table, True
    ).astype(low)
    key_pre_grad = rotate(both_pre[:, :kv_width], cos_table, sin_table, True).astype(low)
    value_pre_grad = both_pre[:, kv_width:].astype(low)
    both_pre_grad = jnp.concatenate([key_pre_grad, value_pre_grad], 1)
    query_wgrad = jnp.einsum("td,tq->dq", normed_one, query_pre_grad, preferred_element_type=wide)
    both_wgrad = jnp.einsum("td,tq->dq", normed_one, both_pre_grad, preferred_element_type=wide)
    normed_one_grad = (
        jnp.einsum("tq,dq->td", query_pre_grad, query_full, preferred_element_type=wide)
        + jnp.einsum("tq,dq->td", key_pre_grad, key_full, preferred_element_type=wide)
        + jnp.einsum("tq,dq->td", value_pre_grad, value_full, preferred_element_type=wide)
    )
    unused_first, first_pull = jax.vjp(rms_norm, input_float, attn_norm_gain)
    input_from_norm, attn_gain_grad = first_pull(normed_one_grad)
    input_grad = middle_grad + input_from_norm

    small = jnp.concatenate(
        [router_wgrad, attn_gain_grad[:, None], moe_gain_grad[:, None]], 1
    ).astype(low)
    small = jnp.pad(small, ((0, 0), (0, -small.shape[1] % 128)))
    batch_sums = [query_wgrad.astype(low), output_wgrad.astype(low), both_wgrad.astype(low), small]
    expert_parts = [
        a.reshape(shard_count, -1, a.shape[1]) for a in (gate_wgrad, up_wgrad, down_wgrad)
    ]
    whole_rows = model_width // shard_count
    if paired and expert_axis & (expert_axis - 1) == 0 and whole_rows % (16 * expert_axis) == 0:
        reduced = reduce_all(batch_sums, expert_parts, expert_axis, 4)
        totals = [a.astype(wide) for a in reduced[:4]]
        expert_sums = [
            own_block(own) + got.astype(wide) for own, got in zip(expert_parts, reduced[4:])
        ]
    else:
        totals = []
        for array in batch_sums:
            part = lax.psum_scatter(array, "shard", scatter_dimension=0, tiled=True)
            totals.append(lax.psum(part, "expert").astype(wide))
        expert_sums = [
            lax.psum_scatter(a, "shard", scatter_dimension=0).astype(wide) for a in expert_parts
        ]
    return (
        layer_out,
        input_grad,
        totals[3][:, expert_count],
        totals[0],
        totals[2][:, :kv_width],
        totals[2][:, kv_width:],
        totals[1],
        totals[3][:, :expert_count],
        totals[3][:, expert_count + 1],
        expert_sums[0][None],
        expert_sums[1][None],
        expert_sums[2][None],
    )


def solution(mesh):
    return jax.shard_map(
        on_device,
        mesh=mesh,
        in_specs=(
            P(("expert", "shard"), None),
            P("expert", None),
            P(("expert", "shard"), None),
            P(),
            P("shard", None),
            P("shard", None),
            P("shard", None),
            P("shard", None),
            P("shard", None),
            P(),
            P("expert", None, None),
            P("expert", None, None),
            P("expert", None, None),
            P(("expert", "shard"), None),
        ),
        out_specs=(
            P(("expert", "shard"), None),
            P(("expert", "shard"), None),
            P("shard"),
            P("shard", None),
            P("shard", None),
            P("shard", None),
            P("shard", None),
            P("shard", None),
            P("shard"),
            P("expert", "shard", None),
            P("expert", "shard", None),
            P("expert", "shard", None),
        ),
        check_vma=False,
    )
```

time: 661 us -> 544 us (0.82); the launches traced: 652 us -> 542 us
  Pallas kernels: 0 us -> 201 us
  waiting for transfers between devices: 325 us -> 160 us
  blocking collectives: 87.5 us -> 0 us
  local copies, waits for them, and re-layouts: 73.7 us -> 36.7 us
  matrix products: 57 us -> 78.6 us
  other arithmetic: 41.2 us -> 20.5 us
  between operations: 16.1 us -> 1.83 us
  starting transfers between devices: 50.9 us -> 43 us
    pallas_call x0 -> x4, Pallas kernels: none -> 201 us  [the longest x2 110 us: gather_pair(): pl.pallas_call(functools.partial(gather_kernel, count), out_shape=[jax.Sh...]
    reduce_scatter x10 -> x0, waiting for transfers between devices: 84.7 us -> none  [the longest x1 13.6 us: on_device(): lax.psum_scatter(output_wgrad.astype(jnp.bfloat16), 'shard', scatter_dime...]
    psum x1 -> x0, blocking collectives: 79 us -> none  [on_device(): lax.psum(shard_sums[5].astype(jnp.bfloat16), 'expert').astype(jnp.float32)]
    psum x1 -> x0, waiting for transfers between devices: 75.3 us -> none  [on_device(): lax.psum(shard_sums[0].astype(jnp.bfloat16), 'expert').astype(jnp.float32)]
    gather x2 -> x0, local copies, waits for them, and re-layouts: 30.4 us -> none  [the longest x1 15.2 us: on_device(): returned[slot_expert, slot_place].reshape(tok_count, TOP, model_width)]
    all_gather x4 -> x0, waiting for transfers between devices: 26.2 us -> none  [the longest x1 8.95 us: on_device(): lax.all_gather(query_weight, 'shard', axis=0, tiled=True)]
    all_to_all x4, waiting for transfers between devices: 136 us -> 160 us  [cross(): lax.all_to_all(values, 'expert', split_axis=0, concat_axis=0, tiled=True)]
    dot_general x20 -> x26, matrix products: 46.3 us -> 62.4 us  [the longest x1 5.54 us: on_device(): up_pre = jnp.dot(flat_rows, up_matrix, preferred_element_type=wide)]
  transfers between devices with their start and end apart: 19 -> 4, of which waited for: 18 -> 4; matrix products, arithmetic and copies ran while one was open for 16% -> 6% of each run, Pallas kernels for 0% -> 0%
where the time goes in v1:
time: 544 us; the launch traced here: 542 us
  Pallas kernels  201 us (37%)
  waiting for transfers between devices  160 us (29%)
  matrix products  78.6 us (14%)
  starting transfers between devices  43 us (8%)
  local copies, waits for them, and re-layouts  36.7 us (7%)
  other arithmetic  20.5 us (4%)
    all_to_all x4, waiting for transfers between devices, cross(): lax.all_to_all(values, 'expert', split_axis=0, concat_axis=0, tiled=True)  160 us
    pallas_call x2, Pallas kernels, gather_pair(): pl.pallas_call(functools.partial(gather_kernel, count), out_shape=[jax.Sh...  110 us
    pallas_call x1, Pallas kernels, reduce_all(): pl.pallas_call(functools.partial(reduce_kernel, levels, parts, swaps), ou...  89.3 us
    all_to_all x4, starting transfers between devices, cross(): lax.all_to_all(values, 'expert', split_axis=0, concat_axis=0, tiled=True)  43 us
  transfers between devices with their start and end apart: 4, of which 4 were waited for; matrix products, arithmetic and copies ran while one was open for 6% of the time, Pallas kernels for 0%

profile of v1, /device:TPU:0, one launch (start us, length us, event | category | flops | bytes accessed | tf_op | source)
XLA Modules:
  0.0 542.0 jit_solution(4501606314744939712)
XLA Ops:
  5.0 1.1 fusion.41
  8.2 100.9 %shard_map.229 = (bf16[2,512,1024]{2,1,0:T(8,128)(2,1)}, bf16[2,512,512]{2,1,0:T(8,128)(2,1)}, bf16[2,512,512]{2,1,0:T(8,128)(2,1)}, bf16[2,512,1024]{2,1,0:T(8,128)(2,1)}, bf16[2,512,128]{2,1,0:T(8,128)(2,1)}) custom-call(bf16[512,1024]{1,0:T(8,128)(2,1)} %refs_0_.1, bf16[512,512]{1,0:T(8,128)(2,1)} %refs_1_.1, bf16[512,512]{1,0:T(8,128)(2,1)} %refs_2_.1, ...), custom_call_target="tpu_custom_call" | custom-call | tf_op jit(solution)/shard_map/pallas_call | solution.py:102
  109.1 1.5 copy.96
  112.1 1.7 convolution_convert_fusion.11
  114.6 9.1 %shard_map.230 = bf16[2,128,1024]{2,1,0:T(8,128)(2,1)} custom-call(bf16[128,1024]{1,0:T(8,128)(2,1)} %pad_maximum_fusion.refs_0_), custom_call_target="tpu_custom_call" | custom-call | tf_op jit(solution)/shard_map/pallas_call | solution.py:102
  123.7 1.1 copy.100
  125.6 1.8 copy.103
  127.5 2.5 copy.104
  130.1 2.5 fusion.56
  135.1 1.5 fusion.8
  136.6 1.5 copy.106
  138.4 2.2 multiply_reduce_fusion.3
  142.5 2.2 convolution_convert_fusion.2
  144.8 8.5 %all-to-all-start.1 = ((bf16[16,72,1024]{2,1,0:T(8,128)(2,1)}), bf16[16,72,1024]{2,1,0:T(8,128)(2,1)}, u32[]{:S(2)}, u32[]{:S(2)}) async-start(bf16[16,72,1024]{2,1,0:T(8,128)(2,1)} %bitcast.219), calls=%async_computation.1 | async-start | bytes 4718592 | tf_op jit(solution)/shard_map/all_to_all | solution.py:325
  153.4 2.3 convolution_convert_fusion
  155.8 45.2 %all-to-all-done.1 = bf16[16,72,1024]{2,1,0:T(8,128)(2,1)} async-done(((bf16[16,72,1024]{2,1,0:T(8,128)(2,1)}), bf16[16,72,1024]{2,1,0:T(8,128)(2,1)}, u32[]{:S(2)}, u32[]{:S(2)}) %all-to-all-start.1) | async-done | bytes 2359328 | tf_op jit(solution)/shard_map/all_to_all | solution.py:325
  201.0 11.5 %all-to-all-start = ((bf16[16,72,1152]{2,1,0:T(8,128)(2,1)}), bf16[16,72,1152]{2,1,0:T(8,128)(2,1)}, u32[]{:S(2)}, u32[]{:S(2)}) async-start(bf16[16,72,1152]{2,1,0:T(8,128)(2,1)} %bitcast.217), calls=%async_computation | async-start | bytes 5308416 | tf_op jit(solution)/shard_map/all_to_all | solution.py:325
  212.5 4.5 fusion.25
  217.0 47.5 %all-to-all-done = bf16[16,72,1152]{2,1,0:T(8,128)(2,1)} async-done(((bf16[16,72,1152]{2,1,0:T(8,128)(2,1)}), bf16[16,72,1152]{2,1,0:T(8,128)(2,1)}, u32[]{:S(2)}, u32[]{:S(2)}) %all-to-all-start) | async-done | bytes 2654240 | tf_op jit(solution)/shard_map/all_to_all | solution.py:325
  265.7 2.4 select_reduce_fusion.1
  268.4 3.3 fusion.31
  271.6 5.5 %multiply_convert_fusion.1 = (bf16[1152,512]{1,0:T(8,128)(2,1)S(1)}, bf16[1152,512]{1,0:T(8,128)(2,1)}, bf16[1152,512]{1,0:T(8,128)(2,1)}) fusion(f32[1152,512]{1,0:T(8,128)S(1)} %copy-done.79, f32[1152,512]{1,0:T(8,128)S(1)} %fusion.31, bf16[1152,1024]{1,0:T(8,128)(2,1)} %bitcast.27, bf16[1,1024,512]{2,1,0:T(8,128)(2,1)S(1)} %copy-done), kind=kOutput, calls=%fused_computation.8 | convolution fusion | flops 1216806912 | bytes 11665408 | tf_op jit(solution)/shard_map/dot_general | solution.py:397
  277.2 2.8 convolution_convert_fusion.1
  280.0 12.1 %all-to-all-start.3 = ((bf16[16,72,1024]{2,1,0:T(8,128)(2,1)}), bf16[16,72,1024]{2,1,0:T(8,128)(2,1)S(1)}, u32[]{:S(2)}, u32[]{:S(2)}) async-start(bf16[16,72,1024]{2,1,0:T(8,128)(2,1)} %bitcast.240), calls=%async_computation.3 | async-start | bytes 4718592 | tf_op jit(solution)/shard_map/all_to_all | solution.py:325
  292.1 3.1 fusion.23
  295.3 2.8 fusion.1
  298.0 41.1 %all-to-all-done.3 = bf16[16,72,1024]{2,1,0:T(8,128)(2,1)S(1)} async-done(((bf16[16,72,1024]{2,1,0:T(8,128)(2,1)}), bf16[16,72,1024]{2,1,0:T(8,128)(2,1)S(1)}, u32[]{:S(2)}, u32[]{:S(2)}) %all-to-all-start.3) | async-done | bytes 2359328 | tf_op jit(solution)/shard_map/all_to_all | solution.py:325
  339.2 1.4 copy-done.2
  340.6 10.9 %all-to-all-start.2 = ((bf16[16,72,1024]{2,1,0:T(8,128)(2,1)}), bf16[16,72,1024]{2,1,0:T(8,128)(2,1)}, u32[]{:S(2)}, u32[]{:S(2)}) async-start(bf16[16,72,1024]{2,1,0:T(8,128)(2,1)} %bitcast.218), calls=%async_computation.2 | async-start | bytes 4718592 | tf_op jit(solution)/shard_map/all_to_all | solution.py:325
  351.8 4.6 convolution_convert_fusion.6
  356.4 3.3 convolution_convert_fusion.7
  359.8 4.4 convolution_convert_fusion.8
  365.2 2.2 convolution_bitcast_fusion.1
  368.2 1.1 fusion.62
  369.3 3.0 fusion.14
  372.2 26.3 %all-to-all-done.2 = bf16[16,72,1024]{2,1,0:T(8,128)(2,1)} async-done(((bf16[16,72,1024]{2,1,0:T(8,128)(2,1)}), bf16[16,72,1024]{2,1,0:T(8,128)(2,1)}, u32[]{:S(2)}, u32[]{:S(2)}) %all-to-all-start.2) | async-done | bytes 2359328 | tf_op jit(solution)/shard_map/all_to_all | solution.py:325
  398.5 3.1 multiply_reduce_fusion.1
  403.1 1.3 copy.111
  404.4 2.0 multiply_reduce_fusion
  406.4 1.2 fusion.17
  408.7 1.0 fusion.18
  410.3 1.2 reshape.399
  411.5 1.0 copy.122
  412.5 1.2 reshape.400
  413.7 1.0 copy.123
  414.8 1.1 maximum_bitcast_fusion
  416.7 1.9 shard_map.231
  418.6 1.1 convert_add_fusion.3
  421.2 2.1 convolution_convert_fusion.4.refs_1_
  423.3 1.8 copy.114
  426.5 1.2 multiply_subtract_fusion.1
  427.8 2.1 convolution_convert_fusion.5.refs_0_
  430.0 1.6 fusion.114
  432.4 1.6 convolution_add_fusion.2
  434.0 1.3 fusion.38
  435.7 2.2 convolution_convert_fusion.3.refs_2_
  437.8 89.3 %shard_map.232 = (bf16[512,1024]{1,0:T(8,128)(2,1)S(1)}, bf16[512,1024]{1,0:T(8,128)(2,1)S(1)}, bf16[512,1024]{1,0:T(8,128)(2,1)S(1)}, bf16[512,128]{1,0:T(8,128...) custom-call(bf16[1024,1024]{1,0:T(8,128)(2,1)} %convolution_convert_fusion.5.r, ...), custom_call_target="tpu_custom_call" | custom-call | tf_op jit(solution)/shard_map/pallas_call | solution.py:261
  528.6 1.1 fusion.20
  529.7 1.6 fusion.108
  531.3 1.6 convert_element_type.291
  532.9 1.6 convert_element_type.293
  534.5 1.7 copy.117
  536.1 2.1 slice_reduce_fusion
  538.2 2.8 fusion.21
  (243 shorter events, 27.9 us)
Async XLA Ops:
  0.6 271.0 %copy-start = (bf16[1,1024,512]{2,1,0:T(8,128)(2,1)S(1)}, bf16[1,1024,512]{2,1,0:T(8,128)(2,1)}, u32[]{:S(2)}) copy-start(bf16[1,1024,512]{2,1,0:T(8,128)(2,1)} %param.25) | copy-start | bytes 3145732
  6.6 104.7 %copy-start.57 = (f32[128]{0:T(128)}, f32[128]{0:T(128)S(1)}, u32[]{:S(2)}) copy-start(f32[128]{0:T(128)S(1)} %fusion.90) | copy-start | bytes 1540
  8.2 103.2 %copy-start.4 = (bf16[128,1024]{1,0:T(8,128)(2,1)S(1)}, bf16[128,1024]{1,0:T(8,128)(2,1)}, u32[]{:S(2)}) copy-start(bf16[128,1024]{1,0:T(8,128)(2,1)} %param.14) | copy-start | bytes 786436
  8.2 103.2 %copy-start.42 = (f32[1024]{0:T(1024)S(1)}, f32[1024]{0:T(1024)}, u32[]{:S(2)}) copy-start(f32[1024]{0:T(1024)} %param.17) | copy-start | bytes 12292
  111.4 21.2 %copy-start.39 = (f32[128,32]{0,1:T(8,128)}, f32[128,32]{0,1:T(8,128)S(1)}, u32[]{:S(2)}) copy-start(f32[128,32]{0,1:T(8,128)S(1)} %get-tuple-element.127) | copy-start | bytes 49156
  112.1 15.3 %copy-start.8 = (bf16[2,512,1024]{2,1,0:T(8,128)(2,1)S(1)}, bf16[2,512,1024]{2,1,0:T(8,128)(2,1)}, u32[]{:S(2)}) copy-start(bf16[2,512,1024]{2,1,0:T(8,128)(2,1)} %get-tuple-element.33) | copy-start | bytes 6291460
  125.6 4.4 copy-start.43
  125.6 4.4 copy-start.58
  130.0 2.9 copy-start.31
  130.0 3.1 copy-start.56
  130.0 3.1 copy-start.68
  130.0 3.1 copy-start.69
  130.0 3.2 copy-start.29
  132.9 3.7 copy-start.36
  133.1 3.5 copy-start.41
  134.1 3.9 copy-start.60
  136.6 4.7 copy-start.67
  136.6 5.3 copy-start.78
  138.1 4.3 copy-start.54
  138.4 4.0 copy-start.24
  140.7 4.1 copy-start.6
  141.3 3.5 copy-start.65
  141.8 11.5 %copy-start.49 = (pred[128,16]{0,1:T(8,128)(4,1)}, pred[128,16]{0,1:T(8,128)(4,1)S(1)}, u32[]{:S(2)}) copy-start(pred[128,16]{0,1:T(8,128)(4,1)S(1)} %get-tuple-element.105) | copy-start | bytes 6148
  144.8 8.7 %copy-start.20 = (bf16[128,1024]{1,0:T(8,128)(2,1)S(1)}, bf16[128,1024]{1,0:T(8,128)(2,1)}, u32[]{:S(2)}) copy-start(bf16[128,1024]{1,0:T(8,128)(2,1)} %param.27) | copy-start | bytes 786436
  144.8 56.2 %all-to-all-start.1 = ((bf16[16,72,1024]{2,1,0:T(8,128)(2,1)}), bf16[16,72,1024]{2,1,0:T(8,128)(2,1)}, u32[]{:S(2)}, u32[]{:S(2)}) async-start(bf16[16,72,1024]{2,1,0:T(8,128)(2,1)} %bitcast.219), calls=%async_computation.1 | async-start | bytes 4718592 | tf_op jit(solution)/shard_map/all_to_all | solution.py:325
  201.0 11.5 %copy-start.76 = (bf16[1,1024,512]{2,1,0:T(8,128)(2,1)S(1)}, bf16[1,1024,512]{2,1,0:T(8,128)(2,1)}, u32[]{:S(2)}) copy-start(bf16[1,1024,512]{2,1,0:T(8,128)(2,1)} %param.24) | copy-start | bytes 3145732
  201.0 63.6 %all-to-all-start = ((bf16[16,72,1152]{2,1,0:T(8,128)(2,1)}), bf16[16,72,1152]{2,1,0:T(8,128)(2,1)}, u32[]{:S(2)}, u32[]{:S(2)}) async-start(bf16[16,72,1152]{2,1,0:T(8,128)(2,1)} %bitcast.217), calls=%async_computation | async-start | bytes 5308416 | tf_op jit(solution)/shard_map/all_to_all | solution.py:325
  212.5 53.2 %copy-start.22 = (bf16[2,512,128]{2,1,0:T(8,128)(2,1)S(1)}, bf16[2,512,128]{2,1,0:T(8,128)(2,1)}, u32[]{:S(2)}) copy-start(bf16[2,512,128]{2,1,0:T(8,128)(2,1)} %get-tuple-element.35) | copy-start | bytes 786436
  217.0 51.3 %copy-start.75 = (bf16[1,512,1024]{2,1,0:T(8,128)(2,1)S(1)}, bf16[1,512,1024]{2,1,0:T(8,128)(2,1)}, u32[]{:S(2)}) copy-start(bf16[1,512,1024]{2,1,0:T(8,128)(2,1)} %param.26) | copy-start | bytes 3145732
  268.3 3.3 copy-start.63
  268.3 3.3 copy-start.79
  277.2 2.8 copy-start.80
  280.0 59.1 %all-to-all-start.3 = ((bf16[16,72,1024]{2,1,0:T(8,128)(2,1)}), bf16[16,72,1024]{2,1,0:T(8,128)(2,1)S(1)}, u32[]{:S(2)}, u32[]{:S(2)}) async-start(bf16[16,72,1024]{2,1,0:T(8,128)(2,1)} %bitcast.240), calls=%async_computation.3 | async-start | bytes 4718592 | tf_op jit(solution)/shard_map/all_to_all | solution.py:325
  292.1 3.1 copy-start.28
  339.1 12.3 %copy-start.16 = (bf16[128,1024]{1,0:T(8,128)(2,1)S(1)}, bf16[128,1024]{1,0:T(8,128)(2,1)}, u32[]{:S(2)}) copy-start(bf16[128,1024]{1,0:T(8,128)(2,1)} %copy-done.15) | copy-start | bytes 786436
  339.1 12.3 %copy-start.23 = (bf16[2,512,128]{2,1,0:T(8,128)(2,1)S(1)}, bf16[2,512,128]{2,1,0:T(8,128)(2,1)}, u32[]{:S(2)}) copy-start(bf16[2,512,128]{2,1,0:T(8,128)(2,1)} %get-tuple-element.35) | copy-start | bytes 786436
  339.1 12.3 %copy-start.50 = (pred[128,16]{0,1:T(8,128)(4,1)S(1)}, pred[128,16]{0,1:T(8,128)(4,1)}, u32[]{:S(2)}) copy-start(pred[128,16]{0,1:T(8,128)(4,1)} %copy-done.49) | copy-start | bytes 6148
  339.1 12.6 %copy-start.72 = (pred[128]{0:T(512)(128)(4,1)S(1)}, pred[128]{0:T(512)(128)(4,1)}, u32[]{:S(2)}) copy-start(pred[128]{0:T(512)(128)(4,1)} %get-tuple-element.104) | copy-start | bytes 388
  340.6 58.0 %all-to-all-start.2 = ((bf16[16,72,1024]{2,1,0:T(8,128)(2,1)}), bf16[16,72,1024]{2,1,0:T(8,128)(2,1)}, u32[]{:S(2)}, u32[]{:S(2)}) async-start(bf16[16,72,1024]{2,1,0:T(8,128)(2,1)} %bitcast.218), calls=%async_computation.2 | async-start | bytes 4718592 | tf_op jit(solution)/shard_map/all_to_all | solution.py:325
  351.8 4.7 copy-start.77
  356.4 3.3 copy-start.64
  356.4 3.3 copy-start.81
  359.8 4.4 copy-start.3
  359.8 4.4 copy-start.21
  365.0 4.2 copy-start.7
  367.4 31.1 %copy-start.55 = (f32[1024]{0:T(1024)S(1)}, f32[1024]{0:T(1024)}, u32[]{:S(2)}) copy-start(f32[1024]{0:T(1024)} %param.23) | copy-start | bytes 12292
  367.4 31.1 %copy-start.66 = (f32[128]{0:T(128)S(1)}, f32[128]{0:T(128)}, u32[]{:S(2)}) copy-start(f32[128]{0:T(128)} %copy-done.65) | copy-start | bytes 1540
  369.3 29.3 %copy-start.26 = (f32[128,1024]{1,0:T(8,128)S(1)}, f32[128,1024]{1,0:T(8,128)}, u32[]{:S(2)}) copy-start(f32[128,1024]{1,0:T(8,128)} %fusion.62) | copy-start | bytes 1572868
  372.2 29.4 %copy-start.74 = (f32[128]{0:T(128)S(1)}, f32[128]{0:T(128)}, u32[]{:S(2)}) copy-start(f32[128]{0:T(128)} %copy-done.73) | copy-start | bytes 1540
  398.5 3.3 copy-start.10
  401.8 19.4 %copy-start.11 = (f32[128,1024]{1,0:T(8,128)}, f32[128,1024]{1,0:T(8,128)S(1)}, u32[]{:S(2)}) copy-start(f32[128,1024]{1,0:T(8,128)S(1)} %fusion.39) | copy-start | bytes 1572868
  414.8 6.4 %copy-start.25 = (bf16[128,1024]{1,0:T(8,128)(2,1)S(1)}, bf16[128,1024]{1,0:T(8,128)(2,1)}, u32[]{:S(2)}) copy-start(bf16[128,1024]{1,0:T(8,128)(2,1)} %copy-done.24) | copy-start | bytes 786436
  419.7 3.5 copy-start.17
  423.3 3.2 copy-start.40
  423.3 3.2 copy-start.45
  426.5 3.5 copy-start.9
  430.0 4.0 copy-start.13
  432.4 2.9 copy-start.62
  432.4 3.0 copy-start.48
  437.8 90.8 %copy-start.19 = (bf16[512,1024]{1,0:T(8,128)(2,1)S(1)}, bf16[512,1024]{1,0:T(8,128)(2,1)}, u32[]{:S(2)}) copy-start(bf16[512,1024]{1,0:T(8,128)(2,1)} %convolution_convert_fusion.8) | copy-start | bytes 3145732
  532.9 5.3 copy-start.71
  536.1 4.9 copy-start.12
  536.1 4.9 copy-start.27
  538.2 3.8 copy-start.1
  (22 other events, 39.1 us)

commit v2 on v1

--- a/solution.py
+++ b/solution.py
@@ -72,40 +72,47 @@
 
 def gather_kernel(count, *refs):
     sources, results = refs[:count], refs[count : 2 * count]
-    send_sem, recv_sem, own_sem = refs[2 * count :]
+    send_sem, recv_sem = refs[2 * count :]
     expert_index, shard_index = lax.axis_index("expert"), lax.axis_index("shard")
     other = (expert_index, 1 - shard_index)
     greet([other])
     copies = []
     for at in range(count):
-        copies.append(
-            pltpu.make_async_remote_copy(
-                src_ref=sources[at],
-                dst_ref=results[at].at[shard_index],
-                send_sem=send_sem.at[at],
-                recv_sem=recv_sem.at[at],
-                device_id=other,
-                device_id_type=MESH_ID,
-            )
+        copy = pltpu.make_async_remote_copy(
+            src_ref=sources[at],
+            dst_ref=results[at].at[shard_index],
+            send_sem=send_sem.at[at],
+            recv_sem=recv_sem.at[at],
+            device_id=other,
+            device_id_type=MESH_ID,
         )
-        copies.append(
-            pltpu.make_async_copy(sources[at], results[at].at[shard_index], own_sem.at[at])
-        )
-    for copy in copies:
         copy.start()
+        copies.append(copy)
+    for at in range(count):
+        step = 32
+
+        def one(index, carry, at=at, step=step):
+            rows = pl.ds(pl.multiple_of(index * step, step), step)
+            results[at][shard_index, rows, :] = sources[at][rows, :]
+            return carry
+
+        lax.fori_loop(0, sources[at].shape[0] // step, one, 0)
     for copy in copies:
         copy.wait()
 
 
 def gather_pair(arrays, identity):
     count = len(arrays)
+    spec = pl.BlockSpec(memory_space=pltpu.VMEM)
     return pl.pallas_call(
         functools.partial(gather_kernel, count),
         out_shape=[jax.ShapeDtypeStruct((2,) + a.shape, a.dtype) for a in arrays],
-        in_specs=[pl.BlockSpec(memory_space=pl.ANY)] * count,
-        out_specs=[pl.BlockSpec(memory_space=pl.ANY)] * count,
-        scratch_shapes=[pltpu.SemaphoreType.DMA((count,))] * 3,
-        compiler_params=pltpu.CompilerParams(collective_id=identity, has_side_effects=True),
+        in_specs=[spec] * count,
+        out_specs=[spec] * count,
+        scratch_shapes=[pltpu.SemaphoreType.DMA((count,))] * 2,
+        compiler_params=pltpu.CompilerParams(
+            collective_id=identity, has_side_effects=True, vmem_limit_bytes=vmem_grant
+        ),
     )(*arrays)
 
 
@@ -136,7 +143,7 @@
     )(array)
 
 
-def add_rows(target, target_at, first, first_at, second, second_at, rows):
+def add_rows(target, target_at, first, first_at, second, second_at, rows, columns):
     step = min(rows, 32)
 
     def one(index, carry):
@@ -144,11 +151,20 @@
         into = pl.ds(pl.multiple_of(target_at + row, step), step)
         left = pl.ds(pl.multiple_of(first_at + row, step), step)
         right = pl.ds(pl.multiple_of(second_at + row, step), step)
-        total = first[left, :].astype(jnp.float32) + second[right, :].astype(jnp.float32)
-        target[into, :] = total.astype(target.dtype)
+        total = first[left, columns].astype(jnp.float32) + second[right, columns].astype(
+            jnp.float32
+        )
+        target[into, columns] = total.astype(target.dtype)
         return carry
 
     lax.fori_loop(0, rows // step, one, 0)
+
+
+def bit_order(array, levels):
+    if levels < 3:
+        return list(range(levels))
+    first = [[0, 1, 2], [1, 2, 0], [2, 0, 1]][array % 3]
+    return first + list(range(3, levels))
 
 
 def reduce_kernel(levels, parts, swaps, *refs):
@@ -161,7 +177,7 @@
 
     sources, swap_sources = take(parts), take(swaps)
     totals, swap_results = take(parts), take(swaps)
-    near, far, held_sums = take(parts), take(parts), take(parts)
+    near, far, partial = take(parts), take(parts), take(parts)
     send_sem, recv_sem, swap_send, swap_recv = refs
     expert_index, shard_index = lax.axis_index("expert"), lax.axis_index("shard")
     other = (expert_index, 1 - shard_index)
@@ -171,13 +187,25 @@
     ]
     greet([other] + partners)
     rows = totals[0].shape[0]
-
-    def send(part, step, source, target, device):
+    lanes = []
+    for piece in range(2):
+        for array in range(parts):
+            width = totals[array].shape[1]
+            if width % 256 == 0:
+                columns = pl.ds(piece * (width // 2), width // 2)
+            elif piece == 0:
+                columns = pl.ds(0, width)
+            else:
+                continue
+            lanes.append((array, columns, bit_order(array, levels)))
+
+    def send(lane, step, source, source_rows, target, target_rows, device):
+        columns = lanes[lane][1]
         copy = pltpu.make_async_remote_copy(
-            src_ref=source,
-            dst_ref=target,
-            send_sem=send_sem.at[part, step],
-            recv_sem=recv_sem.at[part, step],
+            src_ref=source.at[source_rows, columns],
+            dst_ref=target.at[target_rows, columns],
+            send_sem=send_sem.at[lane, step],
+            recv_sem=recv_sem.at[lane, step],
             device_id=device,
             device_id_type=MESH_ID,
         )
@@ -185,9 +213,9 @@
         return copy
 
     flying = []
-    for part in range(parts):
-        away = pl.ds(pl.multiple_of((1 - shard_index) * rows, rows), rows)
-        flying.append(send(part, 0, sources[part].at[away], near[part], other))
+    away = pl.ds(pl.multiple_of((1 - shard_index) * rows, rows), rows)
+    for lane, (array, columns, order) in enumerate(lanes):
+        flying.append(send(lane, 0, sources[array], away, near[array], pl.ds(0, rows), other))
     swapping = []
     for at in range(swaps):
         copy = pltpu.make_async_remote_copy(
@@ -200,53 +228,62 @@
         )
         copy.start()
         swapping.append(copy)
-    starts = [0] * parts
+    starts = [0] * len(lanes)
     size = rows
     landing = 0
     for step in range(2 * levels + 1):
-        for part in range(parts):
-            flying[part].wait()
+        kept = size // 2 if 1 <= step <= levels else size
+        for lane, (array, columns, order) in enumerate(lanes):
+            flying[lane].wait()
             if step == 0:
                 add_rows(
-                    held_sums[part], 0, sources[part], shard_index * rows, near[part], 0, rows
+                    partial[array],
+                    0,
+                    sources[array],
+                    shard_index * rows,
+                    near[array],
+                    0,
+                    rows,
+                    columns,
                 )
             elif step <= levels:
-                bit = (step - 1 + part) % levels
-                starts[part] = starts[part] + held[bit] * (size // 2)
+                starts[lane] = starts[lane] + held[order[step - 1]] * kept
                 add_rows(
-                    totals[part] if step == levels else held_sums[part],
-                    starts[part],
-                    held_sums[part],
-                    starts[part],
-                    far[part],
+                    totals[array] if step == levels else partial[array],
+                    starts[lane],
+                    partial[array],
+                    starts[lane],
+                    far[array],
                     landing,
-                    size // 2,
+                    kept,
+                    columns,
                 )
             else:
-                bit = (2 * levels - step + part) % levels
-                starts[part] = starts[part] - held[bit] * size
+                starts[lane] = starts[lane] - held[order[2 * levels - step]] * size
             if step < levels:
-                half = (size if step == 0 else size // 2) // 2
-                bit = (step + part) % levels
-                leaving = pl.multiple_of(starts[part] + (1 - held[bit]) * half, half)
-                room = 0 if step == 0 else landing + size // 2
-                flying[part] = send(
-                    part,
+                half = kept // 2
+                bit = order[step]
+                leaving = pl.multiple_of(starts[lane] + (1 - held[bit]) * half, half)
+                room = 0 if step == 0 else landing + kept
+                flying[lane] = send(
+                    lane,
                     step + 1,
-                    held_sums[part].at[pl.ds(leaving, half)],
-                    far[part].at[pl.ds(room, half)],
+                    partial[array],
+                    pl.ds(leaving, half),
+                    far[array],
+                    pl.ds(room, half),
                     partners[bit],
                 )
             elif step < 2 * levels:
-                whole = size // 2 if step == levels else size * 2
-                bit = (2 * levels - 1 - step + part) % levels
-                region = pl.ds(pl.multiple_of(starts[part], whole), whole)
-                flying[part] = send(
-                    part, step + 1, totals[part].at[region], totals[part].at[region], partners[bit]
+                whole = kept if step == levels else size * 2
+                region = pl.ds(pl.multiple_of(starts[lane], whole), whole)
+                bit = order[2 * levels - 1 - step]
+                flying[lane] = send(
+                    lane, step + 1, totals[array], region, totals[array], region, partners[bit]
                 )
         if 1 <= step <= levels:
-            landing += size // 2
-            size //= 2
+            landing += kept
+            size = kept
         elif step > levels:
             size *= 2
     for copy in swapping:
@@ -265,7 +302,7 @@
         in_specs=[spec] * (parts + swaps),
         out_specs=[spec] * (parts + swaps),
         scratch_shapes=[pltpu.VMEM((rows, a.shape[1]), a.dtype) for a in list(sources) * 3]
-        + [pltpu.SemaphoreType.DMA((parts, 2 * levels + 1))] * 2
+        + [pltpu.SemaphoreType.DMA((2 * parts, 2 * levels + 1))] * 2
         + [pltpu.SemaphoreType.DMA((swaps,))] * 2,
         compiler_params=pltpu.CompilerParams(
             collective_id=identity, has_side_effects=True, vmem_limit_bytes=vmem_grant
@@ -377,7 +414,8 @@
     branch = jnp.dot(attn_low, output_full, preferred_element_type=wide)
     middle = input_float + res_scale * branch
     normed_two = rms_norm(middle, moe_norm_gain).astype(low)
-    arrived = cross(to_slots(normed_two))
+    send_rows, arrived_top = lax.optimization_barrier((to_slots(normed_two), arrived_top))
+    arrived = cross(send_rows)
 
     def gate_softmax(rows, chosen):
         logits = jnp.dot(rows, router_full, preferred_element_type=wide)

time: 544 us -> 413 us (0.76)
  Pallas kernels: 201 us -> 89.6 us
  waiting for transfers between devices: 160 us -> 105 us
  local copies, waits for them, and re-layouts: 36.7 us -> 52.9 us
  other arithmetic: 20.5 us -> 34.2 us
  matrix products: 78.6 us -> 89.8 us
    pallas_call x2, Pallas kernels: 110 us -> 9.46 us  [gather_pair(): pl.pallas_call(functools.partial(gather_kernel, count), out_shape=[jax.Sh...]
    all_to_all x4, waiting for transfers between devices: 160 us -> 105 us  [cross(): lax.all_to_all(values, 'expert', split_axis=0, concat_axis=0, tiled=True)]
    pallas_call x1, Pallas kernels: 89.3 us -> 78.2 us  [reduce_all(): pl.pallas_call(functools.partial(reduce_kernel, levels, parts, swaps), ou...]
    unnamed x168 -> x140, local copies, waits for them, and re-layouts: 7.6 us -> 11.5 us
  transfers between devices with their start and end apart: 4 -> 4, of which waited for: 4 -> 3; matrix products, arithmetic and copies ran while one was open for 6% -> 20% of each run, Pallas kernels for 0% -> 2%
where the time goes in v2:
time: 413 us; the launch traced here: 411 us
  waiting for transfers between devices  105 us (25%)
  matrix products  89.8 us (22%)
  Pallas kernels  89.6 us (22%)
  local copies, waits for them, and re-layouts  52.9 us (13%)
  starting transfers between devices  38 us (9%)
  other arithmetic  34.2 us (8%)
    all_to_all x4, waiting for transfers between devices, cross(): lax.all_to_all(values, 'expert', split_axis=0, concat_axis=0, tiled=True)  105 us
    pallas_call x1, Pallas kernels, reduce_all(): pl.pallas_call(functools.partial(reduce_kernel, levels, parts, swaps), ou...  78.2 us
    all_to_all x4, starting transfers between devices, cross(): lax.all_to_all(values, 'expert', split_axis=0, concat_axis=0, tiled=True)  38 us
    unnamed x140, local copies, waits for them, and re-layouts  11.5 us
    pallas_call x2, Pallas kernels, gather_pair(): pl.pallas_call(functools.partial(gather_kernel, count), out_shape=[jax.Sh...  9.46 us
  transfers between devices with their start and end apart: 4, of which 3 were waited for; matrix products, arithmetic and copies ran while one was open for 20% of the time, Pallas kernels for 2%

profile of v2, /device:TPU:0, one launch (start us, length us, event | category | flops | bytes accessed | tf_op | source)
XLA Modules:
  0.0 410.7 jit_solution(1159200883341130575)
XLA Ops:
  0.7 1.4 fusion.68
  3.1 3.3 convolution_convert_fusion
  6.4 8.5 %all-to-all-start = ((bf16[16,72,1152]{2,1,0:T(8,128)(2,1)}), bf16[16,72,1152]{2,1,0:T(8,128)(2,1)}, u32[]{:S(2)}, u32[]{:S(2)}) async-start(bf16[16,72,1152]{2,1,0:T(8,128)(2,1)} %bitcast.224), calls=%async_computation | async-start | bytes 5308416 | tf_op jit(solution)/shard_map/all_to_all | solution.py:362
  21.3 7.9 %shard_map.229 = (bf16[2,512,1024]{2,1,0:T(8,128)(2,1)}, bf16[2,512,512]{2,1,0:T(8,128)(2,1)S(1)}, bf16[2,512,512]{2,1,0:T(8,128)(2,1)S(1)}, bf16[2,512,1024]{2,1,0:T(8,128)(2,1)}, bf16[2,512,128]{2,1,0:T(8,128)(2,1)S(1)}) custom-call(bf16[512,1024]{1,0:T(8,128)(2,1)S(1)} %copy-done.4, bf16[512,512]{1,0:T(8,128)(2,1)S(1)} %copy-done.6, ...), custom_call_target="tpu_custom_call" | custom-call | tf_op jit(solution)/shard_map/pallas_call | solution.py:107
  29.2 1.3 copy.94
  31.6 1.4 fusion.86
  33.0 1.9 fusion.58
  35.6 1.7 copy.97
  37.3 1.3 convolution_convert_fusion.11
  39.5 1.6 shard_map.230
  42.0 1.8 copy.101
  43.8 3.9 copy.102
  47.7 2.5 fusion.56
  51.1 2.0 convert_element_type.249
  53.1 1.8 copy.99
  56.4 1.4 compare_and_fusion
  57.7 3.2 fusion.110
  61.0 2.8 fusion.8
  63.7 2.1 copy.104
  65.9 2.2 convert_element_type.253
  68.0 2.9 multiply_reduce_fusion.3
  74.0 2.2 convolution_convert_fusion.2
  76.2 6.9 %all-to-all-start.1 = ((bf16[16,72,1024]{2,1,0:T(8,128)(2,1)}), bf16[16,72,1024]{2,1,0:T(8,128)(2,1)}, u32[]{:S(2)}, u32[]{:S(2)}) async-start(bf16[16,72,1024]{2,1,0:T(8,128)(2,1)} %bitcast.226), calls=%async_computation.1 | async-start | bytes 4718592 | tf_op jit(solution)/shard_map/all_to_all | solution.py:362
  83.6 1.7 slice.88
  85.3 1.7 copy.124
  87.0 43.8 %all-to-all-done.1 = bf16[16,72,1024]{2,1,0:T(8,128)(2,1)} async-done(((bf16[16,72,1024]{2,1,0:T(8,128)(2,1)}), bf16[16,72,1024]{2,1,0:T(8,128)(2,1)}, u32[]{:S(2)}, u32[]{:S(2)}) %all-to-all-start.1) | async-done | bytes 2359328 | tf_op jit(solution)/shard_map/all_to_all | solution.py:362
  130.8 3.6 select_reduce_fusion.1
  134.4 1.3 reduce_or.31
  138.4 3.4 fusion.25
  141.8 3.1 fusion.31
  145.0 5.5 %multiply_convert_fusion.1 = (bf16[1152,512]{1,0:T(8,128)(2,1)S(1)}, bf16[1152,512]{1,0:T(8,128)(2,1)}, bf16[1152,512]{1,0:T(8,128)(2,1)}) fusion(f32[1152,512]{1,0:T(8,128)S(1)} %fusion.25, f32[1152,512]{1,0:T(8,128)S(1)} %fusion.31, bf16[1152,1024]{1,0:T(8,128)(2,1)} %bitcast.27, bf16[1,1024,512]{2,1,0:T(8,128)(2,1)S(1)} %copy-done), kind=kOutput, calls=%fused_computation.8 | convolution fusion | flops 1216806912 | bytes 11665408 | tf_op jit(solution)/shard_map/dot_general | solution.py:435
  150.5 2.8 convolution_convert_fusion.1
  153.4 11.6 %all-to-all-start.3 = ((bf16[16,72,1024]{2,1,0:T(8,128)(2,1)}), bf16[16,72,1024]{2,1,0:T(8,128)(2,1)}, u32[]{:S(2)}, u32[]{:S(2)}) async-start(bf16[16,72,1024]{2,1,0:T(8,128)(2,1)} %bitcast.240), calls=%async_computation.3 | async-start | bytes 4718592 | tf_op jit(solution)/shard_map/all_to_all | solution.py:362
  165.0 3.1 fusion.23
  168.1 2.8 fusion.1
  170.9 41.2 %all-to-all-done.3 = bf16[16,72,1024]{2,1,0:T(8,128)(2,1)} async-done(((bf16[16,72,1024]{2,1,0:T(8,128)(2,1)}), bf16[16,72,1024]{2,1,0:T(8,128)(2,1)}, u32[]{:S(2)}, u32[]{:S(2)}) %all-to-all-start.3) | async-done | bytes 2359328 | tf_op jit(solution)/shard_map/all_to_all | solution.py:362
  212.1 11.0 %all-to-all-start.2 = ((bf16[16,72,1024]{2,1,0:T(8,128)(2,1)}), bf16[16,72,1024]{2,1,0:T(8,128)(2,1)}, u32[]{:S(2)}, u32[]{:S(2)}) async-start(bf16[16,72,1024]{2,1,0:T(8,128)(2,1)} %bitcast.225), calls=%async_computation.2 | async-start | bytes 4718592 | tf_op jit(solution)/shard_map/all_to_all | solution.py:362
  224.1 4.7 %convolution_convert_fusion.6 = bf16[1024,512]{1,0:T(8,128)(2,1)} fusion(bf16[1152,1024]{1,0:T(8,128)(2,1)} %bitcast.27, bf16[1152,512]{1,0:T(8,128)(2,1)} %get-tuple-element.116), kind=kOutput, calls=%fused_computation.17 | convolution fusion | flops 1208483840 | bytes 4587520 | tf_op jit(solution)/shard_map/rd,rf->df/dot_general | solution.py:462
  228.7 3.3 convolution_convert_fusion.7
  232.1 4.7 %convolution_convert_fusion.8 = bf16[512,1024]{1,0:T(8,128)(2,1)} fusion(bf16[1152,512]{1,0:T(8,128)(2,1)S(1)} %copy-done.67, bf16[1152,1152]{1,0:T(8,128)(2,1)} %bitcast.26, f32[1152]{0:T(1024)S(1)} %copy-done.53), kind=kOutput, calls=%fused_computation.19 | convolution fusion | flops 1212022784 | bytes 4592128 | tf_op jit(solution)/shard_map/rf,rd->fd/dot_general | solution.py:458
  236.8 3.3 convolution_multiply_fusion
  240.0 1.7 reduce_sum.177
  243.3 2.2 convolution_bitcast_fusion.1
  247.4 3.0 fusion.14
  250.4 19.8 %all-to-all-done.2 = bf16[16,72,1024]{2,1,0:T(8,128)(2,1)} async-done(((bf16[16,72,1024]{2,1,0:T(8,128)(2,1)}), bf16[16,72,1024]{2,1,0:T(8,128)(2,1)}, u32[]{:S(2)}, u32[]{:S(2)}) %all-to-all-start.2) | async-done | bytes 2359328 | tf_op jit(solution)/shard_map/all_to_all | solution.py:362
  270.2 3.4 multiply_reduce_fusion.1
  277.6 2.2 copy.111
  279.8 2.4 multiply_reduce_fusion
  284.8 1.6 fusion.5
  288.8 2.0 reshape.400
  290.8 1.9 copy.123
  294.5 1.9 shard_map.231
  299.0 3.2 convolution_convert_fusion.4.refs_1_
  303.1 3.1 copy.108
  306.1 2.6 reshape_reshape.3
  311.1 2.1 convolution_convert_fusion.5.refs_0_
  313.2 1.6 fusion.114
  315.6 1.6 convolution_add_fusion.2
  318.9 2.2 convolution_convert_fusion.3.refs_2_
  321.0 78.2 %shard_map.232 = (bf16[512,1024]{1,0:T(8,128)(2,1)S(1)}, bf16[512,1024]{1,0:T(8,128)(2,1)S(1)}, bf16[512,1024]{1,0:T(8,128)(2,1)S(1)}, bf16[512,128]{1,0:T(8,128...) custom-call(bf16[1024,1024]{1,0:T(8,128)(2,1)} %convolution_convert_fusion.5.r, ...), custom_call_target="tpu_custom_call" | custom-call | tf_op jit(solution)/shard_map/pallas_call | solution.py:298
  400.5 1.6 fusion.108
  402.1 1.6 convert_element_type.291
  403.7 1.6 convert_element_type.293
  406.9 2.8 fusion.21
  (216 shorter events, 46.5 us)
Async XLA Ops:
  0.6 144.3 %copy-start = (bf16[1,1024,512]{2,1,0:T(8,128)(2,1)S(1)}, bf16[1,1024,512]{2,1,0:T(8,128)(2,1)}, u32[]{:S(2)}) copy-start(bf16[1,1024,512]{2,1,0:T(8,128)(2,1)} %param.25) | copy-start | bytes 3145732
  2.3 4.2 %copy-start.40 = (s32[16,128]{1,0:T(8,128)}, s32[16,128]{1,0:T(8,128)S(1)}, u32[]{:S(2)}) copy-start(s32[16,128]{1,0:T(8,128)S(1)} %fusion.19) | copy-start | bytes 24580
  6.4 8.5 %copy-start.58 = (s32[2,3]{1,0:T(2,128)S(1)}, s32[2,3]{1,0:T(2,128)}, u32[]{:S(2)}) copy-start(s32[2,3]{1,0:T(2,128)} %param.15) | copy-start | bytes 76
  6.4 10.2 %copy-start.48 = (bf16[512,16]{0,1:T(8,128)(2,1)S(1)}, bf16[512,16]{0,1:T(8,128)(2,1)}, u32[]{:S(2)}) copy-start(bf16[512,16]{0,1:T(8,128)(2,1)} %param.22) | copy-start | bytes 49156
  6.4 69.8 %all-to-all-start = ((bf16[16,72,1152]{2,1,0:T(8,128)(2,1)}), bf16[16,72,1152]{2,1,0:T(8,128)(2,1)}, u32[]{:S(2)}, u32[]{:S(2)}) async-start(bf16[16,72,1152]{2,1,0:T(8,128)(2,1)} %bitcast.224), calls=%async_computation | async-start | bytes 5308416 | tf_op jit(solution)/shard_map/all_to_all | solution.py:362
  14.9 1.0 copy-start.55
  16.7 1.2 copy-start.4
  18.0 1.2 copy-start.5
  19.2 1.0 copy-start.6
  20.2 1.0 copy-start.7
  31.6 1.4 copy-start.59
  31.6 4.0 copy-start.45
  33.0 1.9 copy-start.29
  33.0 2.6 copy-start.35
  47.7 2.5 copy-start.30
  47.7 2.5 copy-start.36
  68.0 4.1 %copy-start.43 = (f32[1024]{0:T(1024)S(1)}, f32[1024]{0:T(1024)}, u32[]{:S(2)}) copy-start(f32[1024]{0:T(1024)} %param.23) | copy-start | bytes 12292
  76.2 54.6 %all-to-all-start.1 = ((bf16[16,72,1024]{2,1,0:T(8,128)(2,1)}), bf16[16,72,1024]{2,1,0:T(8,128)(2,1)}, u32[]{:S(2)}, u32[]{:S(2)}) async-start(bf16[16,72,1024]{2,1,0:T(8,128)(2,1)} %bitcast.226), calls=%async_computation.1 | async-start | bytes 4718592 | tf_op jit(solution)/shard_map/all_to_all | solution.py:362
  138.4 3.4 copy-start.52
  138.4 3.4 copy-start.64
  150.5 2.9 copy-start.66
  153.4 58.7 %all-to-all-start.3 = ((bf16[16,72,1024]{2,1,0:T(8,128)(2,1)}), bf16[16,72,1024]{2,1,0:T(8,128)(2,1)}, u32[]{:S(2)}, u32[]{:S(2)}) async-start(bf16[16,72,1024]{2,1,0:T(8,128)(2,1)} %bitcast.240), calls=%async_computation.3 | async-start | bytes 4718592 | tf_op jit(solution)/shard_map/all_to_all | solution.py:362
  165.0 3.1 copy-start.22
  212.1 11.0 %copy-start.14 = (bf16[128,1024]{1,0:T(8,128)(2,1)S(1)}, bf16[128,1024]{1,0:T(8,128)(2,1)}, u32[]{:S(2)}) copy-start(bf16[128,1024]{1,0:T(8,128)(2,1)} %copy-done.13) | copy-start | bytes 786436
  212.1 11.0 %copy-start.39 = (pred[128,16]{0,1:T(8,128)(4,1)S(1)}, pred[128,16]{0,1:T(8,128)(4,1)}, u32[]{:S(2)}) copy-start(pred[128,16]{0,1:T(8,128)(4,1)} %copy-done.38) | copy-start | bytes 6148
  212.1 11.3 %copy-start.61 = (pred[128]{0:T(512)(128)(4,1)S(1)}, pred[128]{0:T(512)(128)(4,1)}, u32[]{:S(2)}) copy-start(pred[128]{0:T(512)(128)(4,1)} %get-tuple-element.108) | copy-start | bytes 388
  212.1 58.1 %all-to-all-start.2 = ((bf16[16,72,1024]{2,1,0:T(8,128)(2,1)}), bf16[16,72,1024]{2,1,0:T(8,128)(2,1)}, u32[]{:S(2)}, u32[]{:S(2)}) async-start(bf16[16,72,1024]{2,1,0:T(8,128)(2,1)} %bitcast.225), calls=%async_computation.2 | async-start | bytes 4718592 | tf_op jit(solution)/shard_map/all_to_all | solution.py:362
  224.1 4.7 %copy-start.65 = (bf16[1152,512]{1,0:T(8,128)(2,1)S(1)}, bf16[1152,512]{1,0:T(8,128)(2,1)}, u32[]{:S(2)}) copy-start(bf16[1152,512]{1,0:T(8,128)(2,1)} %get-tuple-element.115) | copy-start | bytes 3538948
  228.7 3.3 copy-start.53
  228.7 3.3 copy-start.67
  232.1 88.9 %copy-start.2 = (bf16[1024,512]{1,0:T(8,128)(2,1)}, bf16[1024,512]{1,0:T(8,128)(2,1)S(1)}, u32[]{:S(2)}) copy-start(bf16[1024,512]{1,0:T(8,128)(2,1)S(1)} %convolution_convert_fusion.7) | copy-start | bytes 3145732
  232.1 4.7 %copy-start.19 = (bf16[128,1024]{1,0:T(8,128)(2,1)S(1)}, bf16[128,1024]{1,0:T(8,128)(2,1)}, u32[]{:S(2)}) copy-start(bf16[128,1024]{1,0:T(8,128)(2,1)} %param.27) | copy-start | bytes 786436
  241.7 3.8 copy-start.15
  241.7 5.6 %copy-start.41 = (s32[16,128]{1,0:T(8,128)S(1)}, s32[16,128]{1,0:T(8,128)}, u32[]{:S(2)}) copy-start(s32[16,128]{1,0:T(8,128)} %copy-done.40) | copy-start | bytes 24580
  241.7 5.6 %copy-start.42 = (f32[16,128]{1,0:T(8,128)S(1)}, f32[16,128]{1,0:T(8,128)}, u32[]{:S(2)}) copy-start(f32[16,128]{1,0:T(8,128)} %fusion.83) | copy-start | bytes 24580
  250.4 23.2 %copy-start.20 = (bf16[128,1024]{1,0:T(8,128)(2,1)S(1)}, bf16[128,1024]{1,0:T(8,128)(2,1)}, u32[]{:S(2)}) copy-start(bf16[128,1024]{1,0:T(8,128)(2,1)} %param.27) | copy-start | bytes 786436
  270.2 3.4 copy-start.63
  270.2 3.4 copy-start.44
  270.2 3.4 copy-start.57
  270.2 5.4 %copy-start.10 = (bf16[2,512,1024]{2,1,0:T(8,128)(2,1)S(1)}, bf16[2,512,1024]{2,1,0:T(8,128)(2,1)}, u32[]{:S(2)}) copy-start(bf16[2,512,1024]{2,1,0:T(8,128)(2,1)} %get-tuple-element.36) | copy-start | bytes 6291460
  274.8 0.8 copy-start.11
  275.6 4.1 %copy-start.49 = (f32[2,8,2,64]{3,2,1,0:T(2,128)S(1)}, f32[2,8,2,64]{3,2,1,0:T(2,128)}, u32[]{:S(2)}) copy-start(f32[2,8,2,64]{3,2,1,0:T(2,128)} %get-tuple-element.132) | copy-start | bytes 24580
  279.8 2.4 copy-start.24
  279.8 2.4 copy-start.28
  283.5 1.0 copy-start.27
  283.5 1.4 copy-start.23
  299.0 3.2 slice-start
  302.2 6.5 %copy-start.31 = (f32[128,32]{0,1:T(8,128)S(1)}, f32[128,32]{0,1:T(8,128)}, u32[]{:S(2)}) copy-start(f32[128,32]{0,1:T(8,128)} %copy-done.29) | copy-start | bytes 49156
  302.2 6.5 %copy-start.34 = (f32[128,32]{0,1:T(8,128)S(1)}, f32[128,32]{0,1:T(8,128)}, u32[]{:S(2)}) copy-start(f32[128,32]{0,1:T(8,128)} %get-tuple-element.129) | copy-start | bytes 49156
  303.0 8.0 %copy-start.8 = (bf16[128,1024]{1,0:T(8,128)(2,1)S(1)}, bf16[128,1024]{1,0:T(8,128)(2,1)}, u32[]{:S(2)}) copy-start(bf16[128,1024]{1,0:T(8,128)(2,1)} %param.14) | copy-start | bytes 786436
  303.0 8.0 %copy-start.33 = (f32[1024]{0:T(1024)S(1)}, f32[1024]{0:T(1024)}, u32[]{:S(2)}) copy-start(f32[1024]{0:T(1024)} %param.17) | copy-start | bytes 12292
  303.1 8.0 %copy-start.46 = (f32[128]{0:T(128)S(1)}, f32[128]{0:T(128)}, u32[]{:S(2)}) copy-start(f32[128]{0:T(128)} %copy-done.45) | copy-start | bytes 1540
  308.7 4.5 %copy-start.9 = (bf16[2,512,1024]{2,1,0:T(8,128)(2,1)S(1)}, bf16[2,512,1024]{2,1,0:T(8,128)(2,1)}, u32[]{:S(2)}) copy-start(bf16[2,512,1024]{2,1,0:T(8,128)(2,1)} %get-tuple-element.35) | copy-start | bytes 6291460
  315.6 1.6 copy-start.17
  315.6 2.9 copy-start.50
  315.6 2.9 copy-start.37
  317.2 1.6 copy-start.25
  317.2 1.6 copy-start.26
  321.0 78.3 %copy-start.18 = (bf16[512,1024]{1,0:T(8,128)(2,1)S(1)}, bf16[512,1024]{1,0:T(8,128)(2,1)}, u32[]{:S(2)}) copy-start(bf16[512,1024]{1,0:T(8,128)(2,1)} %convolution_convert_fusion.8) | copy-start | bytes 3145732
  403.7 3.2 copy-start.60
  403.7 3.3 copy-start.3
  405.9 3.8 copy-start.12
  406.0 3.8 copy-start.21
  406.9 3.8 copy-start.1
  (9 other events, 5.9 us)
